TPU v7x, 768 devices: a whole 4x8x12 slice. The times are simulated.
768 devices in a mesh: row: 32 (over y, x), col: 24 (over z, core).
Axes of the slice: x: 4, y: 8, z: 12, core: 2. Of those that a mesh axis runs over, the one named last changes fastest.
Arguments:
- x_stack: float32 [32, 24, 4, 128, 128], P('row', 'col'), may hold values from -6 to 6
- s_stack: float32 [32, 24, 4, 128, 128], P('row', 'col'), may hold values from -0.5 to 0.5
- entries: int32 [32, 24, 2, 4], P('row', 'col'), may hold values from 0 to 7, as said below
- counts: int32 [32, 24], P('row', 'col'), may hold values from 2 to 4, as said below
Outputs:
- y_stack: float32 [32, 24, 4, 128, 128], P('row', 'col')
Inputs may be any that keep to these rules, and one draw needn't show every extreme that they name: `entries`: in every device's stack all 4 slots name distinct blocks of its 6 x 8 region; entry 0 is below 6, entry 1 below 8. `counts`: some device's stack is full.
All inputs are finite; a program needn't handle non-finite values.
Results may differ from a plain program's by a relative error of at most 0.0003.
Values sent between devices are 32-bit elements; how exact they have to be, the bound alone decides.
No kernel may reach another device: no remote copies, remote signals or barrier semaphores. Data moves between devices by JAX's collectives and lax.ppermute only.
A program may use at most 128 MiB of HBM per device.

v0:
```python
import jax
import jax.numpy as jnp
from jax import lax
from jax.sharding import PartitionSpec as P

RB = 6


def per_device(x_stack, s_stack, entries, counts):
    capacity = x_stack.shape[2]
    tile_size = x_stack.shape[3]
    block_rows = RB
    block_cols = RB * lax.axis_size("row") // lax.axis_size("col")
    slot_ids = jnp.arange(capacity, dtype=jnp.int32)
    own_rows = entries[0, 0, 0]
    own_cols = entries[0, 0, 1]
    own_valid = slot_ids < counts[0, 0]
    row_tiles, row_entries, row_counts = (
        lax.all_gather(x_stack, "col", axis=1, tiled=True),
        lax.all_gather(entries, "col", axis=1, tiled=True),
        lax.all_gather(counts, "col", axis=1, tiled=True),
    )
    panel_width = row_tiles.shape[1]
    row_flat = row_tiles.reshape(panel_width * capacity, tile_size, tile_size)
    owners = jnp.arange(panel_width, dtype=jnp.int32)[:, None]
    left_rows = row_entries[0, :, 0].reshape(-1)
    left_inner = (owners * block_cols + row_entries[0, :, 1]).reshape(-1)
    left_valid = (slot_ids[None, :] < row_counts[0][:, None]).reshape(-1)
    positions = jnp.arange(left_rows.shape[0], dtype=jnp.int32)
    col_tiles = lax.all_gather(s_stack, "row", axis=0, tiled=True)
    col_entries = lax.all_gather(entries, "row", axis=0, tiled=True)
    col_counts = lax.all_gather(counts, "row", axis=0, tiled=True)
    piece_rows = col_tiles.shape[0]
    holders = jnp.arange(piece_rows, dtype=jnp.int32)[:, None]
    right_flat = col_tiles.reshape(piece_rows * capacity, tile_size, tile_size)
    right_inner = (holders * block_rows + col_entries[:, 0, 0]).reshape(-1)
    right_cols = col_entries[:, 0, 1].reshape(-1)
    right_valid = (slot_ids[None, :] < col_counts[:, 0][:, None]).reshape(-1)
    matched = (
        (own_rows[:, None, None] == left_rows[None, None, :])
        & (own_cols[:, None, None] == right_cols[None, :, None])
        & (right_inner[None, :, None] == left_inner[None, None, :])
        & right_valid[None, :, None]
        & left_valid[None, None, :]
    )
    chosen_at = jnp.sum(jnp.where(matched, positions, 0), axis=2)
    present = jnp.any(matched, axis=2)
    chosen = jnp.where(present[:, :, None, None], row_flat[chosen_at], 0.0)
    product = jnp.einsum("ofab,fbc->oac", chosen, right_flat, precision=lax.Precision.HIGHEST)
    result = jnp.where(own_valid[:, None, None], 1.5 * x_stack[0, 0] - 0.5 * product, 0.0)
    return result[None, None]


def solution(mesh):
    return jax.shard_map(
        per_device,
        mesh=mesh,
        in_specs=(
            P("row", "col", None, None, None),
            P("row", "col", None, None, None),
            P("row", "col", None, None),
            P("row", "col"),
        ),
        out_specs=P("row", "col", None, None, None),
        check_vma=False,
    )
```

profile of v0, /device:TPU:1, one launch (start us, length us, event | category | flops | bytes accessed | tf_op | source)
XLA Modules:
  0.0 230.4 jit_solution(15972568733873161345)
XLA Ops:
  6.5 0.7 all-gather.3.cloned.1.call-update
  7.3 0.7 all-gather.5.cloned.1.call-update
  8.7 1.3 dynamic-slice
  9.9 0.7 bitcast_dynamic-update-slice_fusion.1
  10.6 17.5 %all-reduce = s32[32]{0:T(128)S(1)} all-reduce(s32[32]{0:T(128)S(1)} %bitcast_dynamic-update-slice_fusion.1), channel_id=1, replica_groups=mesh['row'=32,'col'=24] {'row'}, use_global_device_ids=true, to_apply=%add | all-reduce | flops 32 | bytes 256
  28.1 0.1 iota_compare_fusion
  28.2 0.1 lt.73
  28.3 1.3 dynamic-slice.1
  29.6 0.7 bitcast_dynamic-update-slice_fusion
  30.2 50.5 %all-reduce.1 = s32[24]{0:T(128)S(1)} all-reduce(s32[24]{0:T(128)S(1)} %bitcast_dynamic-update-slice_fusion), channel_id=1, replica_groups=mesh['row'=32,'col'=24] {'col'}, use_global_device_ids=true, to_apply=%add.1 | all-reduce | flops 24 | bytes 192
  80.8 0.1 iota_compare_fusion.1
  80.9 0.1 lt.78
  81.0 28.9 %all_gather.19 = s32[32,1,2,4]{3,2,1,0:T(2,128)S(1)} all-gather(s32[1,1,2,4]{3,2,1,0:T(2,128)} %param.6), channel_id=1, replica_groups=mesh['row'=32,'col'=24] {'row'}, dimensions={0}, use_global_device_ids=true | all-gather | bytes 1056 | tf_op jit(solution)/shard_map/all_gather | solution.py:31
  109.8 0.1 slice_reduce_fusion.1
  109.9 0.1 squeeze.11
  110.0 0.1 add.41
  110.1 0.1 add.42
  110.2 28.3 %all_gather.18 = s32[1,24,2,4]{3,2,0,1:T(2,128)S(1)} all-gather(s32[1,1,2,4]{3,2,0,1:T(2,128)} %bitcast.42), channel_id=1, replica_groups=mesh['row'=32,'col'=24] {'col'}, dimensions={1}, use_global_device_ids=true | all-gather | bytes 800 | tf_op jit(solution)/shard_map/all_gather | solution.py:20
  138.6 0.1 squeeze.12
  138.7 0.1 add.44
  138.7 0.1 add.45
  138.8 0.1 eq.69
  138.9 0.1 eq.64
  139.1 0.8 slice_bitcast_fusion.1
  139.8 0.1 broadcast_compare_fusion.1
  139.9 0.1 broadcast_compare_fusion.2
  140.0 0.1 broadcast_compare_fusion
  140.1 0.1 select_reduce_fusion
  140.3 0.1 fusion.19
  140.4 19.2 %gather_fusion = f32[512,128,128]{2,1,0:T(8,128)} fusion(f32[96,128,128]{2,1,0:T(8,128)} %bitcast.38, s32[1024]{0:T(1024)S(1)} %pad_clamp_fusion), kind=kCustom, calls=%fused_computation | custom fusion | bytes 67110912 | tf_op jit(solution)/shard_map/gather | solution.py:48
  159.7 32.5 %all-gather.5.cloned.1.call-done = f32[32,1,4,128,128]{4,3,2,1,0:T(8,128)} async-done(((f32[1,1,4,128,128]{4,3,2,1,0:T(8,128)}), f32[32,1,4,128,128]{4,3,2,1,0:T(8,128)}) %all-gather.5.cloned.1.call-update) | async-done | bytes 8388624 | tf_op jit(solution)/shard_map/all_gather | solution.py:30
  192.2 31.3 %fusion.16 = f32[1,1,4,128,128]{4,3,2,1,0:T(8,128)} fusion(f32[128,128,128,1]{2,1,0,3:T(8,128)} %bitcast.40, f32[4,128,128,128]{3,2,1,0:T(8,128)} %bitcast.39, pred[4,128]{1,0:T(4,128)(4,1)S(1)} %fusion.19, f32[1,1,4,128,128]{4,3,2,1,0:T(8,128)S(1)} %copy-done, pred[4]{0:T(512)(128)(4,1)S(1)} %iota_compare_fusion.2), kind=kOutput, calls=%fused_computation.9 | convolution fusion | flops 12893552640 | bytes 42467844 | tf_op jit(solution)/shard_map/ofab,fbc->oac/dot_general | solution.py:49
  (15 shorter events, 0.2 us)
Async XLA Ops:
  6.5 133.9 %all-gather.3.cloned.1.call-start = ((), (), s32[]{:S(2)}) async-start(), calls=%async_computation | async-start | bytes 6553600 | tf_op jit(solution)/shard_map/all_gather | solution.py:19
  7.3 184.9 %all-gather.5.cloned.1.call-start = ((), (), s32[]{:S(2)}) async-start(), calls=%async_computation.1 | async-start | bytes 8650752 | tf_op jit(solution)/shard_map/all_gather | solution.py:30
  140.4 51.8 %copy-start = (f32[1,1,4,128,128]{4,3,2,1,0:T(8,128)S(1)}, f32[1,1,4,128,128]{4,3,2,1,0:T(8,128)}, u32[]{:S(2)}) copy-start(f32[1,1,4,128,128]{4,3,2,1,0:T(8,128)} %param.4) | copy-start | bytes 786436
Sparse Core Ops, SparseCore 0:
  9.8 73.1 all-gather.2
  86.8 105.4 all-gather.4
where the time goes:
time: 231 us; the launch traced here: 230 us
  blocking collectives  125 us (54%)
  waiting for transfers between devices  33.9 us (15%)
  matrix products  31.3 us (14%)
  local copies, waits for them, and re-layouts  25 us (11%)
  between operations  14.2 us (6%)
    unnamed x2, blocking collectives  68 us
    all_gather x1, waiting for transfers between devices, per_device(): col_tiles = lax.all_gather(s_stack, 'row', axis=0, tiled=True)  32.5 us
    dot_general x1, matrix products, per_device(): jnp.einsum('ofab,fbc->oac', chosen, right_flat, precision=lax.Precision.H...  31.3 us
    all_gather x1, blocking collectives, per_device(): col_entries = lax.all_gather(entries, 'row', axis=0, tiled=True)  28.9 us
    all_gather x1, blocking collectives, per_device(): lax.all_gather(entries, 'col', axis=1, tiled=True)  28.3 us
    gather x1, local copies, waits for them, and re-layouts, per_device(): chosen = jnp.where(present[:, :, None, None], row_flat[chosen_at], 0.0)  19.2 us
  transfers between devices with their start and end apart: 2, of which 1 were waited for; matrix products, arithmetic and copies ran while one was open for 11% of the time, Pallas kernels for 0%

commit v1 on v0

v1 whole, which is shorter than its diff:
```python
import functools

import jax
import jax.numpy as jnp
from jax import lax
from jax.experimental import pallas as pl
from jax.experimental.pallas import tpu as pltpu
from jax.sharding import PartitionSpec as P

RB = 6
CB = 8
CAP = 4
BS = 128
ROUND = 12

HIGHEST = lax.Precision.HIGHEST
VMEM_LIMIT = 48 * 1024 * 1024


def dot_nt(a, b):
    return lax.dot_general(a, b, (((1,), (1,)), ((), ())), preferred_element_type=jnp.float32)


def pack_kernel(n_row, own_ref, slots_ref, s_ref, out_ref):
    n_col = slots_ref.shape[0]
    rows_out = out_ref.shape[0] // n_row
    piece = BS // n_row
    for e in range(CAP):
        for q in range(piece):
            out_ref[pl.ds(e * piece + q, n_row, stride=rows_out), :] = s_ref[e, q * n_row : (q + 1) * n_row, :]
    slots = slots_ref[...].astype(jnp.float32)
    lane_k = lax.broadcasted_iota(jnp.int32, (n_col, 2 * BS), 1)
    of_col = lax.broadcasted_iota(jnp.int32, (n_col, 2 * BS), 0)
    spread = jnp.where(lane_k // CB == of_col, 1.0, 0.0)
    fields = lax.dot_general(slots, spread, (((0,), (0,)), ((), ())), preferred_element_type=jnp.float32)[:16].astype(jnp.int32)
    k = lax.broadcasted_iota(jnp.int32, (1, 2 * BS), 1)
    within = lax.rem(k, CB)
    owner = lax.div(k, CB)
    held = fields[8:9]
    count = own_ref[8]
    head, tail = [], []
    for o in range(CAP):
        block_row, block_col = own_ref[o], own_ref[CAP + o]
        valid = (o < count).astype(jnp.int32)
        place = jnp.zeros((1, 2 * BS), jnp.int32)
        for e in range(CAP):
            hit = (fields[CAP + e : CAP + e + 1] == within) & (fields[e : e + 1] == block_row) & (e < held)
            place = jnp.where(hit, owner * CAP + e + 1, place)
        place = jnp.where(owner < n_col, place * valid, 0)
        place = jnp.where(k == 192, block_row, place)
        place = jnp.where(k == 193, block_col, place)
        place = jnp.where(k == 194, valid, place)
        head.append(place[:, :BS])
        tail.append(place[:, BS:])
    table = jnp.concatenate(head + tail, axis=0).astype(jnp.float32)
    for m in range(n_row):
        out_ref[m * rows_out + CAP * piece : (m + 1) * rows_out, :] = table


def select_kernel(n_row, where_ref, got_ref, out_ref, plan_ref, m_ref, sel_ref):
    rows_in = got_ref.shape[0] // n_row
    piece = BS // n_row
    base = CAP * piece
    slots = CAP * n_row
    me, first = where_ref[0], where_ref[1]

    def strided(start):
        return got_ref[pl.ds(start, n_row, stride=rows_in), :]

    head = jnp.concatenate([strided(base + o) for o in range(CAP)], axis=0)
    tail = jnp.concatenate([strided(base + CAP + o) for o in range(CAP)], axis=0)
    lane = lax.broadcasted_iota(jnp.int32, (slots, BS), 1)
    holder = lax.rem(lax.broadcasted_iota(jnp.int32, (slots, 1), 0), n_row)
    meta = tail[:, 64:67].astype(jnp.int32)
    inner = holder * RB + meta[:, 0:1]
    block_col = meta[:, 1:2]
    valid = meta[:, 2:3] > 0
    at_head = jnp.where((lane == inner) & valid, 1.0, 0.0)
    at_tail = jnp.where((lane + BS == inner) & valid, 1.0, 0.0)
    of_col = jnp.where(lane == block_col, 1.0, 0.0)
    m = (dot_nt(head, at_head) + dot_nt(tail, at_tail)) * dot_nt(of_col, of_col)
    m_ref[...] = m
    need = m[:n_row]
    for o in range(1, CAP):
        need = jnp.maximum(need, m[o * n_row : (o + 1) * n_row])
    need = jnp.where(need > 0.5, 1.0, 0.0)
    before = jnp.where(
        lax.broadcasted_iota(jnp.int32, (slots, slots), 0) < lax.broadcasted_iota(jnp.int32, (slots, slots), 1), 1.0, 0.0
    )
    rank = jnp.dot(need, before, preferred_element_type=jnp.float32).astype(jnp.int32) - first
    rank = jnp.where(need > 0.5, rank, -1)
    chosen = jnp.concatenate([jnp.where(rank == p, 1.0, 0.0) for p in range(ROUND)], axis=0)
    sel_ref[...] = chosen
    for q in range(piece):
        rows = jnp.concatenate([strided(e * piece + q) for e in range(CAP)], axis=0)
        part = jnp.dot(chosen, rows, precision=HIGHEST, preferred_element_type=jnp.float32)
        for p in range(ROUND):
            out_ref[pl.ds(p * piece + q, n_row, stride=ROUND * piece), :] = part[p * n_row : (p + 1) * n_row]
    row = lax.broadcasted_iota(jnp.int32, (n_row, BS), 0)
    mine = row == me
    own_m = [jnp.sum(jnp.where(mine, m[o * n_row : (o + 1) * n_row], 0.0), axis=0, keepdims=True) for o in range(CAP)]
    own_sel = [
        jnp.sum(jnp.where(mine, chosen[p * n_row : (p + 1) * n_row], 0.0), axis=0, keepdims=True) for p in range(ROUND)
    ]
    pad = [jnp.zeros((BS - ROUND, BS), jnp.float32)]
    plan = dot_nt(jnp.concatenate(own_m + [jnp.zeros((4, BS), jnp.float32)], axis=0), jnp.concatenate(own_sel + pad, axis=0))
    most = jnp.max(jnp.sum(need, axis=1, keepdims=True), axis=0, keepdims=True)
    plan = jnp.where(lax.broadcasted_iota(jnp.int32, (8, BS), 0) == 7, most, plan)
    plan_ref[...] = (plan + 0.5).astype(jnp.int32)


def multiply_kernel(n_row, plan_ref, base_ref, got_ref, x_ref, out_ref, x_buf, sems):
    piece = BS // n_row

    def tile_copy(o, p):
        return pltpu.make_async_copy(x_ref.at[plan_ref[o, p] - 1], x_buf.at[o, p], sems.at[o, p])

    for p in range(ROUND):
        for o in range(CAP):

            @pl.when(plan_ref[o, p] > 0)
            def _():
                tile_copy(o, p).start()

    out_ref[...] = base_ref[...]
    for p in range(ROUND):
        used = plan_ref[0, p]
        for o in range(1, CAP):
            used = used + plan_ref[o, p]

        @pl.when(used > 0)
        def _():
            s_tile = jnp.concatenate(
                [got_ref[pl.ds(p * piece + q, n_row, stride=ROUND * piece), :] for q in range(piece)], axis=0
            )
            for o in range(CAP):

                @pl.when(plan_ref[o, p] > 0)
                def _():
                    tile_copy(o, p).wait()
                    product = jnp.dot(x_buf[o, p], s_tile, precision=HIGHEST, preferred_element_type=jnp.float32)
                    out_ref[o] = out_ref[o] - 0.5 * product


def per_device(n_row, n_col, x_stack, s_stack, entries, counts):
    smem = pl.BlockSpec(memory_space=pltpu.SMEM)
    vmem = pl.BlockSpec(memory_space=pltpu.VMEM)
    params = pltpu.CompilerParams(vmem_limit_bytes=VMEM_LIMIT)
    piece = BS // n_row
    x_own = x_stack[0, 0]
    row_panel = lax.all_gather(x_stack[0], "col", axis=0, tiled=True).reshape(n_col * CAP, BS, BS)

    own = jnp.concatenate([entries.reshape(2 * CAP), counts.reshape(1), jnp.zeros((BS - 2 * CAP - 1,), jnp.int32)])
    slots = lax.all_to_all(jnp.broadcast_to(own[None, None], (n_col, 1, BS)), "col", 0, 0)

    rows_out = CAP * piece + 2 * CAP
    packed = pl.pallas_call(
        functools.partial(pack_kernel, n_row),
        out_shape=jax.ShapeDtypeStruct((n_row * rows_out, BS), jnp.float32),
        in_specs=[smem, vmem, vmem],
        out_specs=vmem,
        compiler_params=params,
        name="pack",
    )(own, slots.reshape(n_col, BS), s_stack[0, 0])
    pieces = lax.all_to_all(packed.reshape(n_row, rows_out, BS), "row", 0, 0).reshape(n_row * rows_out, BS)

    me = lax.axis_index("row").astype(jnp.int32)

    def one_round(first, base):
        chosen, plan = pl.pallas_call(
            functools.partial(select_kernel, n_row),
            out_shape=(
                jax.ShapeDtypeStruct((n_row * ROUND * piece, BS), jnp.float32),
                jax.ShapeDtypeStruct((8, BS), jnp.int32),
            ),
            in_specs=[smem, vmem],
            out_specs=(vmem, vmem),
            scratch_shapes=[pltpu.VMEM((CAP * n_row, BS), jnp.float32), pltpu.VMEM((ROUND * n_row, BS), jnp.float32)],
            compiler_params=params,
            name="select",
        )(jnp.stack([me, first]), pieces)
        tiles = lax.all_to_all(chosen.reshape(n_row, ROUND * piece, BS), "row", 0, 0)
        result = pl.pallas_call(
            functools.partial(multiply_kernel, n_row),
            out_shape=jax.ShapeDtypeStruct((CAP, BS, BS), jnp.float32),
            in_specs=[smem, vmem, vmem, pl.BlockSpec(memory_space=pl.ANY)],
            out_specs=vmem,
            scratch_shapes=[
                pltpu.VMEM((CAP, ROUND, BS, BS), jnp.float32),
                pltpu.SemaphoreType.DMA((CAP, ROUND)),
            ],
            compiler_params=params,
            name="multiply",
        )(plan, base, tiles.reshape(n_row * ROUND * piece, BS), row_panel)
        return plan, result

    valid = jnp.arange(CAP, dtype=jnp.int32) < counts[0, 0]
    base = jnp.where(valid[:, None, None], 1.5 * x_own, 0.0)
    plan, result = one_round(jnp.int32(0), base)
    most = plan[7, 0]

    def another(state):
        first, partial = state
        return first + ROUND, one_round(first, partial)[1]

    _, result = lax.while_loop(lambda state: state[0] < most, another, (jnp.int32(ROUND), result))
    return result[None, None]


def solution(mesh):
    return jax.shard_map(
        functools.partial(per_device, mesh.shape["row"], mesh.shape["col"]),
        mesh=mesh,
        in_specs=(
            P("row", "col", None, None, None),
            P("row", "col", None, None, None),
            P("row", "col", None, None),
            P("row", "col"),
        ),
        out_specs=P("row", "col", None, None, None),
        check_vma=False,
    )
```

time: 231 us -> 102 us (0.44)
  the two profiles are of different devices: /device:TPU:1 before, /device:TPU:4 now
where the time goes in v1:
time: 102 us; the launch traced here: 101 us
  waiting for transfers between devices  34.8 us (34%)
  blocking collectives  25.1 us (25%)
  starting transfers between devices  15.8 us (15%)
  between operations  14.1 us (14%)
  Pallas kernels  6.71 us (7%)
  local copies, waits for them, and re-layouts  2.9 us (3%)
  other arithmetic  1.2 us (1%)
    all_to_all x1, blocking collectives, per_device(): lax.all_to_all(jnp.broadcast_to(own[None, None], (n_col, 1, BS)), 'col',...  25.1 us
    all_to_all x1, waiting for transfers between devices, one_round(): lax.all_to_all(chosen.reshape(n_row, ROUND * piece, BS), 'row', 0, 0)  20.1 us
    all_to_all x1, waiting for transfers between devices, per_device(): lax.all_to_all(packed.reshape(n_row, rows_out, BS), 'row', 0, 0)  14 us
    all_to_all x1, starting transfers between devices, per_device(): lax.all_to_all(packed.reshape(n_row, rows_out, BS), 'row', 0, 0)  10.2 us
    all_to_all x1, starting transfers between devices, one_round(): lax.all_to_all(chosen.reshape(n_row, ROUND * piece, BS), 'row', 0, 0)  5.56 us
    pallas_call x1, Pallas kernels, one_round(): pl.pallas_call(functools.partial(select_kernel, n_row), out_shape=(jax.Sh...  2.75 us
    pallas_call x1, Pallas kernels, one_round(): pl.pallas_call(functools.partial(multiply_kernel, n_row), out_shape=jax.S...  2.43 us
  transfers between devices with their start and end apart: 3, of which 2 were waited for; matrix products, arithmetic and copies ran while one was open for 2% of the time, Pallas kernels for 4%

profile of v1, /device:TPU:4, one launch (start us, length us, event | category | flops | bytes accessed | tf_op | source)
XLA Modules:
  0.0 101.3 jit_solution(6391384159883626912)
XLA Ops:
  6.5 0.0 all-gather.3.cloned.1.call-start
  6.5 0.7 all-gather.3.cloned.1.call-update
  7.9 0.8 reshape.39
  8.7 0.1 pad_add_fusion.2.own_ref
  8.8 25.1 %all_to_all.21 = s32[24,1,128]{2,1,0:T(1,128)S(1)} all-to-all(s32[24,1,128]{2,1,0:T(1,128)S(1)} %broadcast_in_dim.26), channel_id=1, replica_groups=mesh['row'=32,'col'=24] {'col'}, dimensions={0} | all-to-all | bytes 24576 | tf_op jit(solution)/shard_map/all_to_all | solution.py:154
  33.8 0.0 copy-start
  33.8 0.9 copy-done
  34.8 1.5 %pack.1 = f32[768,128]{1,0:T(8,128)} custom-call(s32[128]{0:T(128)S(1)} %pad_add_fusion.2.own_ref, s32[24,128]{1,0:T(8,128)S(1)} %bitcast.31, f32[4,128,128]{2,1,0:T(8,128)S(1)} %bitcast.30), custom_call_target="tpu_custom_call" | custom-call | tf_op jit(solution)/shard_map/pack/pallas_call | solution.py:157
  36.3 10.2 %all-to-all-start.2 = ((f32[32,24,128]{2,1,0:T(8,128)}), f32[32,24,128]{2,1,0:T(8,128)S(1)}, u32[]{:S(2)}, u32[]{:S(2)}) async-start(f32[32,24,128]{2,1,0:T(8,128)} %bitcast.8), calls=%async_computation.2 | async-start | bytes 786432 | tf_op jit(solution)/shard_map/all_to_all | solution.py:165
  46.5 0.1 pad_add_fusion.1.where_ref
  46.6 14.0 %all-to-all-done.2 = f32[32,24,128]{2,1,0:T(8,128)S(1)} async-done(((f32[32,24,128]{2,1,0:T(8,128)}), f32[32,24,128]{2,1,0:T(8,128)S(1)}, u32[]{:S(2)}, u32[]{:S(2)}) %all-to-all-start.2) | async-done | bytes 393248 | tf_op jit(solution)/shard_map/all_to_all | solution.py:165
  60.6 2.8 %select.2 = (f32[1536,128]{1,0:T(8,128)}, s32[8,128]{1,0:T(8,128)S(1)}) custom-call(s32[2]{0:T(128)S(1)} %pad_add_fusion.1.where_ref, f32[768,128]{1,0:T(8,128)S(1)} %bitcast.34), custom_call_target="tpu_custom_call" | custom-call | tf_op jit(solution)/shard_map/select/pallas_call | solution.py:170
  63.3 5.6 %all-to-all-start.3 = ((f32[32,48,128]{2,1,0:T(8,128)}), f32[32,48,128]{2,1,0:T(8,128)S(1)}, u32[]{:S(2)}, u32[]{:S(2)}) async-start(f32[32,48,128]{2,1,0:T(8,128)} %bitcast.12), calls=%async_computation.3 | async-start | bytes 1572864 | tf_op jit(solution)/shard_map/all_to_all | solution.py:182
  68.9 1.0 %bitcast_select_fusion.base_ref = f32[4,128,128]{2,1,0:T(8,128)S(1)} fusion(f32[1,1,4,128,128]{4,3,2,1,0:T(8,128)} %param.6, pred[4]{0:T(512)(128)(4,1)S(1)} %iota_compare_fusion), kind=kLoop, calls=%fused_computation.1 | loop fusion | flops 131072 | bytes 524292 | tf_op jit(solution)/shard_map/jit(_where)/select_n | solution.py:198
  69.9 0.5 slice.3
  70.4 20.1 %all-to-all-done.3 = f32[32,48,128]{2,1,0:T(8,128)S(1)} async-done(((f32[32,48,128]{2,1,0:T(8,128)}), f32[32,48,128]{2,1,0:T(8,128)S(1)}, u32[]{:S(2)}, u32[]{:S(2)}) %all-to-all-start.3) | async-done | bytes 786464 | tf_op jit(solution)/shard_map/all_to_all | solution.py:182
  90.5 0.0 all-gather.3.cloned.1.call-done
  90.5 2.4 %multiply.2 = f32[4,128,128]{2,1,0:T(8,128)S(1)} custom-call(s32[8,128]{1,0:T(8,128)S(1)} %get-tuple-element.42.plan_ref, f32[4,128,128]{2,1,0:T(8,128)S(1)} %bitcast_select_fusion.base_ref, f32[1536,128]{1,0:T(8,128)S(1)} %bitcast.29, f32[96,128,128]{2,1,0:T(8,128)} %bitcast.32), custom_call_target="tpu_custom_call" | custom-call | tf_op jit(solution)/shard_map/multiply/pallas_call | solution.py:183
  93.0 0.7 while.10
  93.7 0.0 copy-start.1
  93.7 0.7 copy-done.1
  (3 shorter events, 0.0 us)
Async XLA Ops:
  6.5 84.0 %all-gather.3.cloned.1.call-start = ((), (), s32[]{:S(2)}) async-start(), calls=%async_computation.4 | async-start | bytes 6553600 | tf_op jit(solution)/shard_map/all_gather | solution.py:151
  33.8 1.0 copy-start
  36.3 24.3 %all-to-all-start.2 = ((f32[32,24,128]{2,1,0:T(8,128)}), f32[32,24,128]{2,1,0:T(8,128)S(1)}, u32[]{:S(2)}, u32[]{:S(2)}) async-start(f32[32,24,128]{2,1,0:T(8,128)} %bitcast.8), calls=%async_computation.2 | async-start | bytes 786432 | tf_op jit(solution)/shard_map/all_to_all | solution.py:165
  63.3 27.2 %all-to-all-start.3 = ((f32[32,48,128]{2,1,0:T(8,128)}), f32[32,48,128]{2,1,0:T(8,128)S(1)}, u32[]{:S(2)}, u32[]{:S(2)}) async-start(f32[32,48,128]{2,1,0:T(8,128)} %bitcast.12), calls=%async_computation.3 | async-start | bytes 1572864 | tf_op jit(solution)/shard_map/all_to_all | solution.py:182
  93.7 0.7 copy-start.1
Sparse Core Ops, SparseCore 0:
  9.8 72.2 all-gather.2

commit v2 on v1

v2 whole, which is shorter than its diff:
```python
import functools

import jax
import jax.numpy as jnp
from jax import lax
from jax.experimental import pallas as pl
from jax.experimental.pallas import tpu as pltpu
from jax.sharding import PartitionSpec as P

RB = 6
CB = 8
CAP = 4
BS = 128
ROUND = 12
TABLE = 2

VMEM_LIMIT = 48 * 1024 * 1024


def iota(shape, dim):
    return lax.broadcasted_iota(jnp.int32, shape, dim)


def dot(a, b, dims=((1,), (0,))):
    return lax.dot_general(a, b, (dims, ((), ())), preferred_element_type=jnp.float32)


def split(a, parts):
    out = []
    for _ in range(parts):
        out.append(a.astype(jnp.bfloat16))
        a = a - out[-1].astype(jnp.float32)
    return out


def cut_kernel(n_row, s_ref, out_ref):
    piece = BS // n_row
    rows_out = CAP * piece + TABLE
    for e in range(CAP):
        for q in range(piece):
            out_ref[pl.ds(e * piece + q, n_row, stride=rows_out), :] = s_ref[e, q * n_row : (q + 1) * n_row, :]
    for t in range(TABLE):
        out_ref[pl.ds(CAP * piece + t, n_row, stride=rows_out), :] = jnp.zeros((n_row, BS), jnp.float32)


def pack_kernel(n_row, n_col, slots_ref, cut_ref, out_ref):
    piece = BS // n_row
    rows_out = CAP * piece + TABLE
    out_ref[...] = cut_ref[...]
    of_slot = lax.rem(iota((BS, BS), 1), CAP)
    field = iota((BS, BS), 0)
    mine = iota((n_col, BS), 0) == lax.div(iota((n_col, BS), 1), CAP)
    got = slots_ref[...].reshape(n_col, BS).astype(jnp.float32)

    def along(at):
        spread = jnp.where(field == at, 1.0, 0.0)
        return jnp.sum(jnp.where(mine, dot(got, spread), 0.0), axis=0, keepdims=True)

    used = lax.rem(iota((1, BS), 1), CAP).astype(jnp.float32) < along(2 * CAP)
    block_row = jnp.where(used, along(of_slot), -1.0)
    block_col = along(of_slot + CAP)
    out_ref[pl.ds(CAP * piece, n_row, stride=rows_out), :] = jnp.broadcast_to(block_row, (n_row, BS))
    out_ref[pl.ds(CAP * piece + 1, n_row, stride=rows_out), :] = jnp.broadcast_to(block_col, (n_row, BS))


def select_kernel(n_row, first_ref, got_ref, out_ref, plan_ref):
    piece = BS // n_row
    rows_in = CAP * piece + TABLE
    base = CAP * piece
    slots = CAP * n_row
    my_row, my_col, first = lax.axis_index("row"), lax.axis_index("col"), first_ref[0]

    def strided(start):
        return got_ref[pl.ds(start, n_row, stride=rows_in), :]

    block_row, block_col = strided(base), strided(base + 1)
    lane = iota((n_row, BS), 1)
    own_row, own_col = [], []
    for o in range(CAP):
        here = lane == my_col * CAP + o
        own_row.append(jnp.sum(jnp.where(here, block_row, 0.0), axis=1, keepdims=True))
        own_col.append(jnp.sum(jnp.where(here, block_col, 0.0), axis=1, keepdims=True))
    both = jnp.concatenate([block_row, block_col], axis=0)
    of_slot, of_k = iota((BS, 2 * BS), 0), iota((BS, 2 * BS), 1)
    k = iota((n_row, 2 * BS), 1)
    within = lax.rem(k, CB).astype(jnp.float32)
    place = (lax.div(k, CB) * CAP + 1).astype(jnp.float32)
    spread = [dot(both, jnp.where(of_slot == lax.div(of_k, CB) * CAP + e, 1.0, 0.0)) for e in range(CAP)]
    in_col = [spread[e][n_row:] == within for e in range(CAP)]
    tables = []
    for o in range(CAP):
        wanted = jnp.where(own_row[o] < 0.0, -2.0, own_row[o])
        found = jnp.zeros((n_row, 2 * BS), jnp.float32)
        for e in range(CAP):
            found = jnp.where(in_col[e] & (spread[e][:n_row] == wanted), place + e, found)
        tables.append(found)
    table = jnp.concatenate(tables, axis=0)
    holds_row = jnp.concatenate(own_row, axis=0).astype(jnp.int32)
    holds_col = jnp.concatenate(own_col, axis=0).astype(jnp.int32)
    inner = lax.rem(iota((slots, 1), 0), n_row) * RB + holds_row
    valid = holds_row >= 0
    wide = iota((slots, BS), 1)
    at_head = jnp.where((wide == inner) & valid, 1.0, 0.0)
    at_tail = jnp.where((wide + BS == inner) & valid, 1.0, 0.0)
    of_col = jnp.where(wide == holds_col, 1.0, 0.0)
    nt = ((1,), (1,))
    m = (dot(table[:, :BS], at_head, nt) + dot(table[:, BS:], at_tail, nt)) * dot(of_col, of_col, nt)
    need = m[:n_row]
    for o in range(1, CAP):
        need = jnp.maximum(need, m[o * n_row : (o + 1) * n_row])
    need = jnp.where(need > 0.5, 1.0, 0.0)
    before = jnp.where(iota((slots, slots), 0) < iota((slots, slots), 1), 1.0, 0.0)
    rank = dot(need, before).astype(jnp.int32) - first
    rank = jnp.where(need > 0.5, rank, -1)
    chosen = jnp.concatenate([jnp.where(rank == p, 1.0, 0.0) for p in range(ROUND)], axis=0)
    rows = jnp.concatenate(
        [jnp.concatenate([strided(e * piece + q) for e in range(CAP)], axis=0) for q in range(piece)], axis=1
    )
    pick = chosen.astype(jnp.bfloat16)
    high, mid, low = split(rows, 3)
    part = dot(pick, high) + dot(pick, mid) + dot(pick, low)
    for q in range(piece):
        for p in range(ROUND):
            out_ref[pl.ds(p * piece + q, n_row, stride=ROUND * piece), :] = part[
                p * n_row : (p + 1) * n_row, q * BS : (q + 1) * BS
            ]
    mine = iota((n_row, BS), 0) == my_row

    def own(a, n):
        return [jnp.sum(jnp.where(mine, a[i * n_row : (i + 1) * n_row], 0.0), axis=0, keepdims=True) for i in range(n)]

    own_m = jnp.concatenate(own(m, CAP) + [jnp.zeros((4, BS), jnp.float32)], axis=0)
    own_chosen = jnp.concatenate(own(chosen, ROUND) + [jnp.zeros((BS - ROUND, BS), jnp.float32)], axis=0)
    most = jnp.max(jnp.sum(need, axis=1, keepdims=True), axis=0, keepdims=True)
    plan = jnp.where(iota((8, BS), 0) == 7, most, dot(own_m, own_chosen, nt))
    plan_ref[...] = (plan + 0.5).astype(jnp.int32)


def multiply_kernel(n_row, plan_ref, base_ref, got_ref, x_ref, out_ref, x_buf, sems):
    piece = BS // n_row

    def tile_copy(o, p):
        return pltpu.make_async_copy(x_ref.at[plan_ref[o, p] - 1], x_buf.at[o, p], sems.at[o, p])

    for p in range(ROUND):
        for o in range(CAP):

            @pl.when(plan_ref[o, p] > 0)
            def _():
                tile_copy(o, p).start()

    out_ref[...] = base_ref[...]
    for p in range(ROUND):
        used = plan_ref[0, p]
        for o in range(1, CAP):
            used = used + plan_ref[o, p]

        @pl.when(used > 0)
        def _():
            s_tile = jnp.concatenate(
                [got_ref[pl.ds(p * piece + q, n_row, stride=ROUND * piece), :] for q in range(piece)], axis=0
            )
            s_high, s_low = split(s_tile, 2)
            for o in range(CAP):

                @pl.when(plan_ref[o, p] > 0)
                def _():
                    tile_copy(o, p).wait()
                    x_high, x_low = split(x_buf[o, p], 2)
                    product = dot(x_high, s_high) + (dot(x_high, s_low) + dot(x_low, s_high))
                    out_ref[o] = out_ref[o] - 0.5 * product


def per_device(n_row, n_col, x_stack, s_stack, entries, counts):
    smem = pl.BlockSpec(memory_space=pltpu.SMEM)
    vmem = pl.BlockSpec(memory_space=pltpu.VMEM)
    hbm = pl.BlockSpec(memory_space=pltpu.HBM)
    params = pltpu.CompilerParams(vmem_limit_bytes=VMEM_LIMIT)
    piece = BS // n_row
    rows_out = CAP * piece + TABLE
    x_own = x_stack[0, 0]
    row_panel = lax.all_gather(x_stack[0], "col", axis=0, tiled=True).reshape(n_col * CAP, BS, BS)

    own = jnp.concatenate([entries.reshape(2 * CAP), counts.reshape(1), jnp.zeros((BS - 2 * CAP - 1,), jnp.int32)])
    slots = lax.all_to_all(jnp.broadcast_to(own[None, None], (n_col, 1, BS)), "col", 0, 0)
    cut = pl.pallas_call(
        functools.partial(cut_kernel, n_row),
        out_shape=jax.ShapeDtypeStruct((n_row * rows_out, BS), jnp.float32),
        in_specs=[vmem],
        out_specs=vmem,
        compiler_params=params,
        cost_estimate=pl.CostEstimate(flops=0, bytes_accessed=2**22, transcendentals=0),
        name="cut",
    )(s_stack[0, 0])
    packed = pl.pallas_call(
        functools.partial(pack_kernel, n_row, n_col),
        out_shape=jax.ShapeDtypeStruct((n_row * rows_out, BS), jnp.float32),
        in_specs=[vmem, vmem],
        out_specs=vmem,
        compiler_params=params,
        name="pack",
    )(slots, cut)
    parts = rows_out // 2
    pieces = lax.all_to_all(packed.reshape(n_row, parts, 2, BS), "row", 0, 0).reshape(n_row * rows_out, BS)

    def one_round(first, base):
        chosen, plan = pl.pallas_call(
            functools.partial(select_kernel, n_row),
            out_shape=(
                jax.ShapeDtypeStruct((n_row * ROUND * piece, BS), jnp.float32),
                jax.ShapeDtypeStruct((8, BS), jnp.int32),
            ),
            in_specs=[smem, vmem],
            out_specs=(vmem, vmem),
            compiler_params=params,
            name="select",
        )(first.reshape(1), pieces)
        tiles = lax.all_to_all(chosen.reshape(n_row, ROUND * piece, BS), "row", 0, 0)
        result = pl.pallas_call(
            functools.partial(multiply_kernel, n_row),
            out_shape=jax.ShapeDtypeStruct((CAP, BS, BS), jnp.float32),
            in_specs=[smem, vmem, vmem, hbm],
            out_specs=vmem,
            scratch_shapes=[
                pltpu.VMEM((CAP, ROUND, BS, BS), jnp.float32),
                pltpu.SemaphoreType.DMA((CAP, ROUND)),
            ],
            compiler_params=params,
            name="multiply",
        )(plan, base, tiles.reshape(n_row * ROUND * piece, BS), row_panel)
        return plan, result

    valid = jnp.arange(CAP, dtype=jnp.int32) < counts[0, 0]
    base = jnp.where(valid[:, None, None], 1.5 * x_own, 0.0)
    plan, result = one_round(jnp.zeros((), jnp.int32), base)
    most = plan[7, 0]

    def another(state):
        first, partial = state
        return first + ROUND, one_round(first, partial)[1]

    _, result = lax.while_loop(lambda state: state[0] < most, another, (jnp.int32(ROUND), result))
    return result[None, None]


def solution(mesh):
    return jax.shard_map(
        functools.partial(per_device, mesh.shape["row"], mesh.shape["col"]),
        mesh=mesh,
        in_specs=(
            P("row", "col", None, None, None),
            P("row", "col", None, None, None),
            P("row", "col", None, None),
            P("row", "col"),
        ),
        out_specs=P("row", "col", None, None, None),
        check_vma=False,
    )
```

time: 102 us -> 97.1 us (0.952)
  the two profiles are of different devices: /device:TPU:4 before, /device:TPU:2 now
where the time goes in v2:
time: 97.1 us; the launch traced here: 96.7 us
  waiting for transfers between devices  29.6 us (30%)
  blocking collectives  22 us (23%)
  starting transfers between devices  20.9 us (22%)
  between operations  14.1 us (15%)
  Pallas kernels  4.78 us (5%)
  local copies, waits for them, and re-layouts  3.54 us (4%)
  other arithmetic  1.12 us (1%)
    all_to_all x1, blocking collectives, per_device(): lax.all_to_all(packed.reshape(n_row, parts, 2, BS), 'row', 0, 0)  22 us
    all_to_all x1, waiting for transfers between devices, one_round(): lax.all_to_all(chosen.reshape(n_row, ROUND * piece, BS), 'row', 0, 0)  20.1 us
    all_to_all x1, starting transfers between devices, per_device(): lax.all_to_all(jnp.broadcast_to(own[None, None], (n_col, 1, BS)), 'col',...  15.4 us
    all_to_all x1, waiting for transfers between devices, per_device(): lax.all_to_all(jnp.broadcast_to(own[None, None], (n_col, 1, BS)), 'col',...  8.84 us
    all_to_all x1, starting transfers between devices, one_round(): lax.all_to_all(chosen.reshape(n_row, ROUND * piece, BS), 'row', 0, 0)  5.57 us
    pallas_call x1, Pallas kernels, one_round(): pl.pallas_call(functools.partial(multiply_kernel, n_row), out_shape=jax.S...  2.57 us
    pallas_call x1, Pallas kernels, one_round(): pl.pallas_call(functools.partial(select_kernel, n_row), out_shape=(jax.Sh...  2.06 us
  transfers between devices with their start and end apart: 3, of which 2 were waited for; matrix products, arithmetic and copies ran while one was open for 3% of the time, Pallas kernels for 2%

profile of v2, /device:TPU:2, one launch (start us, length us, event | category | flops | bytes accessed | tf_op | source)
XLA Modules:
  0.0 96.7 jit_solution(5849600913319446911)
XLA Ops:
  6.5 0.0 all-gather.3.cloned.1.call-start
  6.5 0.7 all-gather.3.cloned.1.call-update
  7.9 0.8 reshape.39
  8.7 0.1 pad_add_fusion
  8.7 0.6 broadcast_in_dim.26
  9.4 15.4 %all-to-all-start.1 = ((s32[24,1,128]{2,1,0:T(1,128)}), s32[24,1,128]{2,1,0:T(1,128)S(1)}, u32[]{:S(2)}, u32[]{:S(2)}) async-start(s32[24,1,128]{2,1,0:T(1,128)} %broadcast_in_dim.26), calls=%async_computation.1 | async-start | bytes 24576 | tf_op jit(solution)/shard_map/all_to_all | solution.py:185
  24.7 0.0 copy-start
  24.7 0.9 copy-done
  25.7 8.8 %all-to-all-done.1.slots_ref = s32[24,1,128]{2,1,0:T(1,128)S(1)} async-done(((s32[24,1,128]{2,1,0:T(1,128)}), s32[24,1,128]{2,1,0:T(1,128)S(1)}, u32[]{:S(2)}, u32[]{:S(2)}) %all-to-all-start.1) | async-done | bytes 12320 | tf_op jit(solution)/shard_map/all_to_all | solution.py:185
  34.5 0.1 pack.1
  34.7 22.0 %all_to_all.21 = f32[32,9,2,128]{3,2,1,0:T(2,128)S(1)} all-to-all(f32[32,9,2,128]{3,2,1,0:T(2,128)S(1)} %bitcast.25), channel_id=1, replica_groups=mesh['row'=32,'col'=24] {'row'}, dimensions={0} | all-to-all | bytes 589824 | tf_op jit(solution)/shard_map/all_to_all | solution.py:204
  56.7 2.1 %select.2 = (f32[1536,128]{1,0:T(8,128)}, s32[8,128]{1,0:T(8,128)S(1)}) custom-call(s32[1]{0:T(128)} %constant.2.clone.1.first_ref, f32[576,128]{1,0:T(8,128)S(1)} %bitcast.29), custom_call_target="tpu_custom_call" | custom-call | tf_op jit(solution)/shard_map/select/pallas_call | solution.py:207
  58.7 5.6 %all-to-all-start.3 = ((f32[32,48,128]{2,1,0:T(8,128)}), f32[32,48,128]{2,1,0:T(8,128)S(1)}, u32[]{:S(2)}, u32[]{:S(2)}) async-start(f32[32,48,128]{2,1,0:T(8,128)} %bitcast.9), calls=%async_computation.3 | async-start | bytes 1572864 | tf_op jit(solution)/shard_map/all_to_all | solution.py:218
  64.3 1.0 %bitcast_select_fusion.base_ref = f32[4,128,128]{2,1,0:T(8,128)S(1)} fusion(f32[1,1,4,128,128]{4,3,2,1,0:T(8,128)} %param.6, pred[4]{0:T(512)(128)(4,1)S(1)} %iota_compare_fusion), kind=kLoop, calls=%fused_computation | loop fusion | flops 131072 | bytes 524292 | tf_op jit(solution)/shard_map/jit(_where)/select_n | solution.py:234
  65.4 0.5 slice.3
  65.9 20.1 %all-to-all-done.3 = f32[32,48,128]{2,1,0:T(8,128)S(1)} async-done(((f32[32,48,128]{2,1,0:T(8,128)}), f32[32,48,128]{2,1,0:T(8,128)S(1)}, u32[]{:S(2)}, u32[]{:S(2)}) %all-to-all-start.3) | async-done | bytes 786464 | tf_op jit(solution)/shard_map/all_to_all | solution.py:218
  86.0 0.0 all-gather.3.cloned.1.call-done
  86.0 2.6 %multiply.2 = f32[4,128,128]{2,1,0:T(8,128)S(1)} custom-call(s32[8,128]{1,0:T(8,128)S(1)} %get-tuple-element.37.plan_ref, f32[4,128,128]{2,1,0:T(8,128)S(1)} %bitcast_select_fusion.base_ref, f32[1536,128]{1,0:T(8,128)S(1)} %bitcast.24, f32[96,128,128]{2,1,0:T(8,128)} %bitcast.27), custom_call_target="tpu_custom_call" | custom-call | tf_op jit(solution)/shard_map/multiply/pallas_call | solution.py:219
  88.5 0.6 while.10
  89.2 0.0 copy-start.1
  89.2 0.7 copy-done.1
  (3 shorter events, 0.0 us)
Async XLA Ops:
  6.5 79.4 %all-gather.3.cloned.1.call-start = ((), (), s32[]{:S(2)}) async-start(), calls=%async_computation.4 | async-start | bytes 6553600 | tf_op jit(solution)/shard_map/all_gather | solution.py:182
  9.4 25.2 %all-to-all-start.1 = ((s32[24,1,128]{2,1,0:T(1,128)}), s32[24,1,128]{2,1,0:T(1,128)S(1)}, u32[]{:S(2)}, u32[]{:S(2)}) async-start(s32[24,1,128]{2,1,0:T(1,128)} %broadcast_in_dim.26), calls=%async_computation.1 | async-start | bytes 24576 | tf_op jit(solution)/shard_map/all_to_all | solution.py:185
  24.7 1.0 copy-start
  58.7 27.2 %all-to-all-start.3 = ((f32[32,48,128]{2,1,0:T(8,128)}), f32[32,48,128]{2,1,0:T(8,128)S(1)}, u32[]{:S(2)}, u32[]{:S(2)}) async-start(f32[32,48,128]{2,1,0:T(8,128)} %bitcast.9), calls=%async_computation.3 | async-start | bytes 1572864 | tf_op jit(solution)/shard_map/all_to_all | solution.py:218
  89.2 0.7 copy-start.1
Sparse Core Ops, SparseCore 0:
  9.8 72.2 all-gather.2

commit v3 on v2

--- a/solution.py
+++ b/solution.py
@@ -12,9 +12,10 @@
 CAP = 4
 BS = 128
 ROUND = 12
+AHEAD = 16
 TABLE = 2
 
-VMEM_LIMIT = 48 * 1024 * 1024
+VMEM_LIMIT = 24 * 1024 * 1024
 
 
 def iota(shape, dim):
@@ -43,7 +44,7 @@
         out_ref[pl.ds(CAP * piece + t, n_row, stride=rows_out), :] = jnp.zeros((n_row, BS), jnp.float32)
 
 
-def pack_kernel(n_row, n_col, slots_ref, cut_ref, out_ref):
+def pack_kernel(n_row, n_col, slots_ref, cut_ref, ahead_ref, out_ref):
     piece = BS // n_row
     rows_out = CAP * piece + TABLE
     out_ref[...] = cut_ref[...]
@@ -63,7 +64,7 @@
     out_ref[pl.ds(CAP * piece + 1, n_row, stride=rows_out), :] = jnp.broadcast_to(block_col, (n_row, BS))
 
 
-def select_kernel(n_row, first_ref, got_ref, out_ref, plan_ref):
+def select_kernel(n_row, first_ref, got_ref, out_ref, plan_ref, most_ref):
     piece = BS // n_row
     rows_in = CAP * piece + TABLE
     base = CAP * piece
@@ -131,44 +132,71 @@
 
     own_m = jnp.concatenate(own(m, CAP) + [jnp.zeros((4, BS), jnp.float32)], axis=0)
     own_chosen = jnp.concatenate(own(chosen, ROUND) + [jnp.zeros((BS - ROUND, BS), jnp.float32)], axis=0)
-    most = jnp.max(jnp.sum(need, axis=1, keepdims=True), axis=0, keepdims=True)
-    plan = jnp.where(iota((8, BS), 0) == 7, most, dot(own_m, own_chosen, nt))
+    needed = jnp.sum(need, axis=1, keepdims=True)
+    most_ref[0, 0] = (jnp.max(needed) + 0.5).astype(jnp.int32)
+    here = jnp.sum(jnp.sum(own_chosen, axis=1, keepdims=True), axis=0, keepdims=True)
+    plan = jnp.where(iota((8, BS), 0) == 7, here, dot(own_m, own_chosen, nt))
     plan_ref[...] = (plan + 0.5).astype(jnp.int32)
 
 
-def multiply_kernel(n_row, plan_ref, base_ref, got_ref, x_ref, out_ref, x_buf, sems):
-    piece = BS // n_row
-
-    def tile_copy(o, p):
-        return pltpu.make_async_copy(x_ref.at[plan_ref[o, p] - 1], x_buf.at[o, p], sems.at[o, p])
-
-    for p in range(ROUND):
+def each_product(plan_ref, act):
+    def tile(p, n):
         for o in range(CAP):
-
-            @pl.when(plan_ref[o, p] > 0)
+            used = plan_ref[o, p] > 0
+
+            @pl.when(used)
             def _():
-                tile_copy(o, p).start()
-
+                act(n, o, p)
+
+            n = n + used.astype(jnp.int32)
+        return n
+
+    lax.fori_loop(0, plan_ref[7, 0], tile, 0)
+
+
+def fetch_kernel(plan_ref, x_ref, out_ref, sems):
+    def copy(n, o, p):
+        return pltpu.make_async_copy(x_ref.at[plan_ref[o, p] - 1], out_ref.at[n], sems.at[n])
+
+    def start(n, o, p):
+        @pl.when(n < AHEAD)
+        def _():
+            copy(n, o, p).start()
+
+    def wait(n, o, p):
+        @pl.when(n < AHEAD)
+        def _():
+            copy(n, o, p).wait()
+
+    each_product(plan_ref, start)
+    each_product(plan_ref, wait)
+
+
+def multiply_kernel(n_row, plan_ref, base_ref, got_ref, ahead_ref, x_ref, out_ref, x_buf, sem):
+    piece = BS // n_row
     out_ref[...] = base_ref[...]
-    for p in range(ROUND):
-        used = plan_ref[0, p]
-        for o in range(1, CAP):
-            used = used + plan_ref[o, p]
-
-        @pl.when(used > 0)
-        def _():
-            s_tile = jnp.concatenate(
-                [got_ref[pl.ds(p * piece + q, n_row, stride=ROUND * piece), :] for q in range(piece)], axis=0
-            )
-            s_high, s_low = split(s_tile, 2)
-            for o in range(CAP):
-
-                @pl.when(plan_ref[o, p] > 0)
-                def _():
-                    tile_copy(o, p).wait()
-                    x_high, x_low = split(x_buf[o, p], 2)
-                    product = dot(x_high, s_high) + (dot(x_high, s_low) + dot(x_low, s_high))
-                    out_ref[o] = out_ref[o] - 0.5 * product
+
+    def act(n, o, p):
+        s_tile = jnp.concatenate(
+            [got_ref[pl.ds(p * piece + q, n_row, stride=ROUND * piece), :] for q in range(piece)], axis=0
+        )
+        s_high, s_low = split(s_tile, 2)
+
+        @pl.when(n < AHEAD)
+        def _():
+            x_buf[...] = ahead_ref[jnp.minimum(n, AHEAD - 1)]
+
+        @pl.when(n >= AHEAD)
+        def _():
+            copy = pltpu.make_async_copy(x_ref.at[plan_ref[o, p] - 1], x_buf, sem)
+            copy.start()
+            copy.wait()
+
+        x_high, x_low = split(x_buf[...], 2)
+        product = dot(x_high, s_high) + (dot(x_high, s_low) + dot(x_low, s_high))
+        out_ref[o] = out_ref[o] - 0.5 * product
+
+    each_product(plan_ref, act)
 
 
 def per_device(n_row, n_col, x_stack, s_stack, entries, counts):
@@ -181,6 +209,8 @@
     x_own = x_stack[0, 0]
     row_panel = lax.all_gather(x_stack[0], "col", axis=0, tiled=True).reshape(n_col * CAP, BS, BS)
 
+    valid = jnp.arange(CAP, dtype=jnp.int32) < counts[0, 0]
+    base = jnp.where(valid[:, None, None], 1.5 * x_own, 0.0)
     own = jnp.concatenate([entries.reshape(2 * CAP), counts.reshape(1), jnp.zeros((BS - 2 * CAP - 1,), jnp.int32)])
     slots = lax.all_to_all(jnp.broadcast_to(own[None, None], (n_col, 1, BS)), "col", 0, 0)
     cut = pl.pallas_call(
@@ -195,50 +225,59 @@
     packed = pl.pallas_call(
         functools.partial(pack_kernel, n_row, n_col),
         out_shape=jax.ShapeDtypeStruct((n_row * rows_out, BS), jnp.float32),
-        in_specs=[vmem, vmem],
+        in_specs=[vmem, vmem, pl.BlockSpec(memory_space=pl.ANY)],
         out_specs=vmem,
         compiler_params=params,
         name="pack",
-    )(slots, cut)
+    )(slots, cut, base)
     parts = rows_out // 2
     pieces = lax.all_to_all(packed.reshape(n_row, parts, 2, BS), "row", 0, 0).reshape(n_row * rows_out, BS)
 
-    def one_round(first, base):
-        chosen, plan = pl.pallas_call(
+    def select(first):
+        chosen, plan, most = pl.pallas_call(
             functools.partial(select_kernel, n_row),
             out_shape=(
                 jax.ShapeDtypeStruct((n_row * ROUND * piece, BS), jnp.float32),
                 jax.ShapeDtypeStruct((8, BS), jnp.int32),
+                jax.ShapeDtypeStruct((1, 1), jnp.int32),
             ),
             in_specs=[smem, vmem],
-            out_specs=(vmem, vmem),
+            out_specs=(vmem, vmem, smem),
             compiler_params=params,
             name="select",
         )(first.reshape(1), pieces)
         tiles = lax.all_to_all(chosen.reshape(n_row, ROUND * piece, BS), "row", 0, 0)
-        result = pl.pallas_call(
+        return tiles.reshape(n_row * ROUND * piece, BS), plan, most[0, 0]
+
+    def multiply(tiles, plan, base):
+        x_tiles = pl.pallas_call(
+            fetch_kernel,
+            out_shape=jax.ShapeDtypeStruct((AHEAD, BS, BS), jnp.float32),
+            in_specs=[smem, hbm],
+            out_specs=vmem,
+            scratch_shapes=[pltpu.SemaphoreType.DMA((AHEAD,))],
+            compiler_params=params,
+            cost_estimate=pl.CostEstimate(flops=0, bytes_accessed=2**23, transcendentals=0),
+            name="fetch",
+        )(plan, row_panel)
+        return pl.pallas_call(
             functools.partial(multiply_kernel, n_row),
             out_shape=jax.ShapeDtypeStruct((CAP, BS, BS), jnp.float32),
-            in_specs=[smem, vmem, vmem, hbm],
+            in_specs=[smem, vmem, vmem, vmem, hbm],
             out_specs=vmem,
-            scratch_shapes=[
-                pltpu.VMEM((CAP, ROUND, BS, BS), jnp.float32),
-                pltpu.SemaphoreType.DMA((CAP, ROUND)),
-            ],
+            scratch_shapes=[pltpu.VMEM((BS, BS), jnp.float32), pltpu.SemaphoreType.DMA],
             compiler_params=params,
             name="multiply",
-        )(plan, base, tiles.reshape(n_row * ROUND * piece, BS), row_panel)
-        return plan, result
-
-    valid = jnp.arange(CAP, dtype=jnp.int32) < counts[0, 0]
-    base = jnp.where(valid[:, None, None], 1.5 * x_own, 0.0)
-    plan, result = one_round(jnp.zeros((), jnp.int32), base)
-    most = plan[7, 0]
+        )(plan, base, tiles, x_tiles, row_panel)
+
+    tiles, plan, most = select(jnp.zeros((), jnp.int32))
 
     def another(state):
         first, partial = state
-        return first + ROUND, one_round(first, partial)[1]
-
+        more, where, _ = select(first)
+        return first + ROUND, multiply(more, where, partial)
+
+    result = multiply(tiles, plan, base)
     _, result = lax.while_loop(lambda state: state[0] < most, another, (jnp.int32(ROUND), result))
     return result[None, None]
 

time: 97.1 us -> 96.2 us (level)
  the two profiles are of different devices: /device:TPU:2 before, /device:TPU:4 now
where the time goes in v3:
time: 96.2 us; the launch traced here: 95.7 us
  waiting for transfers between devices  28.4 us (30%)
  blocking collectives  22 us (23%)
  starting transfers between devices  20.9 us (22%)
  between operations  14.1 us (15%)
  Pallas kernels  5.54 us (6%)
  local copies, waits for them, and re-layouts  3.01 us (3%)
  other arithmetic  1.12 us (1%)
    all_to_all x1, blocking collectives, per_device(): lax.all_to_all(packed.reshape(n_row, parts, 2, BS), 'row', 0, 0)  22 us
    all_gather x1, waiting for transfers between devices, per_device(): lax.all_gather(x_stack[0], 'col', axis=0, tiled=True)  17.7 us
    all_to_all x1, starting transfers between devices, per_device(): lax.all_to_all(jnp.broadcast_to(own[None, None], (n_col, 1, BS)), 'col',...  15.4 us
    all_to_all x1, waiting for transfers between devices, per_device(): lax.all_to_all(jnp.broadcast_to(own[None, None], (n_col, 1, BS)), 'col',...  7.8 us
    all_to_all x1, starting transfers between devices, select(): lax.all_to_all(chosen.reshape(n_row, ROUND * piece, BS), 'row', 0, 0)  5.57 us
    all_to_all x1, waiting for transfers between devices, select(): lax.all_to_all(chosen.reshape(n_row, ROUND * piece, BS), 'row', 0, 0)  2.18 us
    pallas_call x1, Pallas kernels, select(): pl.pallas_call(functools.partial(select_kernel, n_row), out_shape=(jax.Sh...  2.08 us
  transfers between devices with their start and end apart: 3, of which 3 were waited for; matrix products, arithmetic and copies ran while one was open for 3% of the time, Pallas kernels for 4%

profile of v3, /device:TPU:4, one launch (start us, length us, event | category | flops | bytes accessed | tf_op | source)
XLA Modules:
  0.0 95.7 jit_solution(11817260834165521126)
XLA Ops:
  6.5 0.0 all-gather.3.cloned.1.call-start
  6.5 0.7 all-gather.3.cloned.1.call-update
  7.9 0.8 reshape.39
  8.7 0.1 pad_add_fusion
  8.7 0.6 broadcast_in_dim.26
  9.4 15.4 %all-to-all-start.1 = ((s32[24,1,128]{2,1,0:T(1,128)}), s32[24,1,128]{2,1,0:T(1,128)S(1)}, u32[]{:S(2)}, u32[]{:S(2)}) async-start(s32[24,1,128]{2,1,0:T(1,128)} %broadcast_in_dim.26), calls=%async_computation.1 | async-start | bytes 24576 | tf_op jit(solution)/shard_map/all_to_all | solution.py:215
  24.7 1.0 %bitcast_select_fusion.ahead_ref.base_ref = f32[4,128,128]{2,1,0:T(8,128)S(1)} fusion(f32[1,1,4,128,128]{4,3,2,1,0:T(8,128)} %param.6, pred[4]{0:T(512)(128)(4,1)S(1)} %iota_compare_fusion), kind=kLoop, calls=%fused_computation | loop fusion | flops 131072 | bytes 524292 | tf_op jit(solution)/shard_map/jit(_where)/select_n | solution.py:213
  25.8 0.0 copy-start
  25.8 0.9 copy-done
  26.8 7.8 %all-to-all-done.1.slots_ref = s32[24,1,128]{2,1,0:T(1,128)S(1)} async-done(((s32[24,1,128]{2,1,0:T(1,128)}), s32[24,1,128]{2,1,0:T(1,128)S(1)}, u32[]{:S(2)}, u32[]{:S(2)}) %all-to-all-start.1) | async-done | bytes 12320 | tf_op jit(solution)/shard_map/all_to_all | solution.py:215
  34.6 0.1 pack.1
  34.7 22.0 %all_to_all.21 = f32[32,9,2,128]{3,2,1,0:T(2,128)S(1)} all-to-all(f32[32,9,2,128]{3,2,1,0:T(2,128)S(1)} %bitcast.25), channel_id=1, replica_groups=mesh['row'=32,'col'=24] {'row'}, dimensions={0} | all-to-all | bytes 589824 | tf_op jit(solution)/shard_map/all_to_all | solution.py:234
  56.7 2.1 %select.2 = (f32[1536,128]{1,0:T(8,128)}, s32[8,128]{1,0:T(8,128)S(1)}, s32[1,1]{1,0:T(1,128)}) custom-call(s32[1]{0:T(128)} %constant.2.clone.1.first_ref, f32[576,128]{1,0:T(8,128)S(1)} %bitcast.30), custom_call_target="tpu_custom_call" | custom-call | tf_op jit(solution)/shard_map/select/pallas_call | solution.py:237
  58.7 5.6 %all-to-all-start.3 = ((f32[32,48,128]{2,1,0:T(8,128)}), f32[32,48,128]{2,1,0:T(8,128)S(1)}, u32[]{:S(2)}, u32[]{:S(2)}) async-start(f32[32,48,128]{2,1,0:T(8,128)} %bitcast.9), calls=%async_computation.3 | async-start | bytes 1572864 | tf_op jit(solution)/shard_map/all_to_all | solution.py:249
  64.3 17.7 %all-gather.3.cloned.1.call-done = f32[24,1,4,128,128]{4,3,2,1,0:T(8,128)} async-done(((f32[1,1,4,128,128]{4,3,2,1,0:T(8,128)}), f32[24,1,4,128,128]{4,3,2,1,0:T(8,128)}) %all-gather.3.cloned.1.call-update) | async-done | bytes 6291472 | tf_op jit(solution)/shard_map/all_gather | solution.py:210
  82.1 1.7 %fetch.2.ahead_ref = f32[16,128,128]{2,1,0:T(8,128)S(1)} custom-call(s32[8,128]{1,0:T(8,128)S(1)} %get-tuple-element.38.plan_ref, f32[96,128,128]{2,1,0:T(8,128)} %bitcast.27), custom_call_target="tpu_custom_call" | custom-call | bytes 8388608 | tf_op jit(solution)/shard_map/fetch/pallas_call | solution.py:253
  83.8 2.2 %all-to-all-done.3 = f32[32,48,128]{2,1,0:T(8,128)S(1)} async-done(((f32[32,48,128]{2,1,0:T(8,128)}), f32[32,48,128]{2,1,0:T(8,128)S(1)}, u32[]{:S(2)}, u32[]{:S(2)}) %all-to-all-start.3) | async-done | bytes 786464 | tf_op jit(solution)/shard_map/all_to_all | solution.py:249
  86.0 1.6 %multiply.2 = f32[4,128,128]{2,1,0:T(8,128)S(1)} custom-call(s32[8,128]{1,0:T(8,128)S(1)} %get-tuple-element.38.plan_ref, f32[4,128,128]{2,1,0:T(8,128)S(1)} %bitcast_select_fusion.ahead_ref.base_ref, f32[1536,128]{1,0:T(8,128)S(1)} %bitcast.24, f32[16,128,128]{2,1,0:T(8,128)S(1)} %fetch.2.ahead_ref, f32[96,128,128]{2,1,0:T(8,128)} %bitcast.28), custom_call_target="tpu_custom_call" | custom-call | tf_op jit(solution)/shard_map/multiply/pallas_call | solution.py:263
  87.6 0.6 while.10
  88.2 0.0 copy-start.1
  88.2 0.7 copy-done.1
  (3 shorter events, 0.0 us)
Async XLA Ops:
  6.5 75.5 %all-gather.3.cloned.1.call-start = ((), (), s32[]{:S(2)}) async-start(), calls=%async_computation.4 | async-start | bytes 6553600 | tf_op jit(solution)/shard_map/all_gather | solution.py:210
  9.4 25.2 %all-to-all-start.1 = ((s32[24,1,128]{2,1,0:T(1,128)}), s32[24,1,128]{2,1,0:T(1,128)S(1)}, u32[]{:S(2)}, u32[]{:S(2)}) async-start(s32[24,1,128]{2,1,0:T(1,128)} %broadcast_in_dim.26), calls=%async_computation.1 | async-start | bytes 24576 | tf_op jit(solution)/shard_map/all_to_all | solution.py:215
  25.8 1.0 copy-start
  58.7 27.2 %all-to-all-start.3 = ((f32[32,48,128]{2,1,0:T(8,128)}), f32[32,48,128]{2,1,0:T(8,128)S(1)}, u32[]{:S(2)}, u32[]{:S(2)}) async-start(f32[32,48,128]{2,1,0:T(8,128)} %bitcast.9), calls=%async_computation.3 | async-start | bytes 1572864 | tf_op jit(solution)/shard_map/all_to_all | solution.py:249
  88.2 0.7 copy-start.1
Sparse Core Ops, SparseCore 0:
  9.8 72.2 all-gather.2

commit v4 on v3

--- a/solution.py
+++ b/solution.py
@@ -64,12 +64,13 @@
     out_ref[pl.ds(CAP * piece + 1, n_row, stride=rows_out), :] = jnp.broadcast_to(block_col, (n_row, BS))
 
 
-def select_kernel(n_row, first_ref, got_ref, out_ref, plan_ref, most_ref):
+def select_kernel(n_row, initial, *refs):
+    got_ref, out_ref, plan_ref, most_ref = refs[-4:]
     piece = BS // n_row
     rows_in = CAP * piece + TABLE
     base = CAP * piece
     slots = CAP * n_row
-    my_row, my_col, first = lax.axis_index("row"), lax.axis_index("col"), first_ref[0]
+    my_row, my_col, first = lax.axis_index("row"), lax.axis_index("col"), 0 if initial else refs[0][0]
 
     def strided(start):
         return got_ref[pl.ds(start, n_row, stride=rows_in), :]
@@ -117,9 +118,8 @@
     rows = jnp.concatenate(
         [jnp.concatenate([strided(e * piece + q) for e in range(CAP)], axis=0) for q in range(piece)], axis=1
     )
-    pick = chosen.astype(jnp.bfloat16)
-    high, mid, low = split(rows, 3)
-    part = dot(pick, high) + dot(pick, mid) + dot(pick, low)
+    pick = jnp.concatenate([chosen.astype(jnp.bfloat16)] * 3, axis=1)
+    part = dot(pick, jnp.concatenate(split(rows, 3), axis=0))
     for q in range(piece):
         for p in range(ROUND):
             out_ref[pl.ds(p * piece + q, n_row, stride=ROUND * piece), :] = part[
@@ -233,24 +233,24 @@
     parts = rows_out // 2
     pieces = lax.all_to_all(packed.reshape(n_row, parts, 2, BS), "row", 0, 0).reshape(n_row * rows_out, BS)
 
-    def select(first):
+    def select(*first):
         chosen, plan, most = pl.pallas_call(
-            functools.partial(select_kernel, n_row),
+            functools.partial(select_kernel, n_row, not first),
             out_shape=(
                 jax.ShapeDtypeStruct((n_row * ROUND * piece, BS), jnp.float32),
                 jax.ShapeDtypeStruct((8, BS), jnp.int32),
                 jax.ShapeDtypeStruct((1, 1), jnp.int32),
             ),
-            in_specs=[smem, vmem],
+            in_specs=[smem] * len(first) + [vmem],
             out_specs=(vmem, vmem, smem),
             compiler_params=params,
             name="select",
-        )(first.reshape(1), pieces)
+        )(*first, pieces)
         tiles = lax.all_to_all(chosen.reshape(n_row, ROUND * piece, BS), "row", 0, 0)
         return tiles.reshape(n_row * ROUND * piece, BS), plan, most[0, 0]
 
-    def multiply(tiles, plan, base):
-        x_tiles = pl.pallas_call(
+    def fetch(plan):
+        return pl.pallas_call(
             fetch_kernel,
             out_shape=jax.ShapeDtypeStruct((AHEAD, BS, BS), jnp.float32),
             in_specs=[smem, hbm],
@@ -260,6 +260,8 @@
             cost_estimate=pl.CostEstimate(flops=0, bytes_accessed=2**23, transcendentals=0),
             name="fetch",
         )(plan, row_panel)
+
+    def multiply(tiles, plan, base, x_tiles):
         return pl.pallas_call(
             functools.partial(multiply_kernel, n_row),
             out_shape=jax.ShapeDtypeStruct((CAP, BS, BS), jnp.float32),
@@ -270,15 +272,22 @@
             name="multiply",
         )(plan, base, tiles, x_tiles, row_panel)
 
-    tiles, plan, most = select(jnp.zeros((), jnp.int32))
+    tiles, plan, most = select()
 
     def another(state):
         first, partial = state
-        more, where, _ = select(first)
-        return first + ROUND, multiply(more, where, partial)
-
-    result = multiply(tiles, plan, base)
-    _, result = lax.while_loop(lambda state: state[0] < most, another, (jnp.int32(ROUND), result))
+        more, where, _ = select(first.reshape(1))
+        return first + ROUND, multiply(more, where, partial, fetch(where))
+
+    x_tiles = fetch(plan)
+    result = lax.cond(
+        most > ROUND,
+        lambda ahead: lax.while_loop(
+            lambda state: state[0] < most, another, (jnp.int32(ROUND), multiply(tiles, plan, base, ahead))
+        )[1],
+        lambda ahead: multiply(tiles, plan, base, ahead),
+        x_tiles,
+    )
     return result[None, None]
 
 

time: 96.2 us -> 95.3 us (level)
  the two profiles are of different devices: /device:TPU:4 before, /device:TPU:2 now
where the time goes in v4:
time: 95.3 us; the launch traced here: 95 us
  waiting for transfers between devices  27.7 us (29%)
  blocking collectives  22 us (23%)
  starting transfers between devices  21 us (22%)
  between operations  14.8 us (16%)
  Pallas kernels  6.12 us (6%)
  local copies, waits for them, and re-layouts  2.32 us (2%)
  other arithmetic  1.12 us (1%)
    all_to_all x1, blocking collectives, per_device(): lax.all_to_all(packed.reshape(n_row, parts, 2, BS), 'row', 0, 0)  22 us
    all_gather x1, waiting for transfers between devices, per_device(): lax.all_gather(x_stack[0], 'col', axis=0, tiled=True)  17.2 us
    all_to_all x1, starting transfers between devices, per_device(): lax.all_to_all(jnp.broadcast_to(own[None, None], (n_col, 1, BS)), 'col',...  15.4 us
    all_to_all x1, waiting for transfers between devices, per_device(): lax.all_to_all(jnp.broadcast_to(own[None, None], (n_col, 1, BS)), 'col',...  7.78 us
    all_to_all x1, starting transfers between devices, select(): lax.all_to_all(chosen.reshape(n_row, ROUND * piece, BS), 'row', 0, 0)  5.58 us
    pallas_call x1, Pallas kernels, multiply(): pl.pallas_call(functools.partial(multiply_kernel, n_row), out_shape=jax.S...  2.29 us
    all_to_all x1, waiting for transfers between devices, select(): lax.all_to_all(chosen.reshape(n_row, ROUND * piece, BS), 'row', 0, 0)  2.07 us
    pallas_call x1, Pallas kernels, select(): pl.pallas_call(functools.partial(select_kernel, n_row, not first), out_sh...  1.96 us
  transfers between devices with their start and end apart: 3, of which 3 were waited for; matrix products, arithmetic and copies ran while one was open for 3% of the time, Pallas kernels for 4%

profile of v4, /device:TPU:2, one launch (start us, length us, event | category | flops | bytes accessed | tf_op | source)
XLA Modules:
  0.0 95.0 jit_solution(10631101292379552901)
XLA Ops:
  6.5 0.0 all-gather.3.cloned.1.call-start
  6.5 0.7 all-gather.3.cloned.1.call-update
  7.9 0.8 reshape.39
  8.7 0.1 pad_add_fusion
  8.7 0.6 broadcast_in_dim.30
  9.4 15.4 %all-to-all-start.1 = ((s32[24,1,128]{2,1,0:T(1,128)}), s32[24,1,128]{2,1,0:T(1,128)S(1)}, u32[]{:S(2)}, u32[]{:S(2)}) async-start(s32[24,1,128]{2,1,0:T(1,128)} %broadcast_in_dim.30), calls=%async_computation.1 | async-start | bytes 24576 | tf_op jit(solution)/shard_map/all_to_all | solution.py:215
  24.7 1.0 %bitcast_select_fusion.ahead_ref = f32[4,128,128]{2,1,0:T(8,128)S(1)} fusion(f32[1,1,4,128,128]{4,3,2,1,0:T(8,128)} %param.8, pred[4]{0:T(512)(128)(4,1)S(1)} %iota_compare_fusion), kind=kLoop, calls=%fused_computation | loop fusion | flops 131072 | bytes 524292 | tf_op jit(solution)/shard_map/jit(_where)/select_n | solution.py:213
  25.8 0.0 copy-start
  25.8 0.9 copy-done
  26.8 7.8 %all-to-all-done.1.slots_ref = s32[24,1,128]{2,1,0:T(1,128)S(1)} async-done(((s32[24,1,128]{2,1,0:T(1,128)}), s32[24,1,128]{2,1,0:T(1,128)S(1)}, u32[]{:S(2)}, u32[]{:S(2)}) %all-to-all-start.1) | async-done | bytes 12320 | tf_op jit(solution)/shard_map/all_to_all | solution.py:215
  34.5 0.1 pack.1
  34.7 22.0 %all_to_all.21 = f32[32,9,2,128]{3,2,1,0:T(2,128)S(1)} all-to-all(f32[32,9,2,128]{3,2,1,0:T(2,128)S(1)} %bitcast.25), channel_id=1, replica_groups=mesh['row'=32,'col'=24] {'row'}, dimensions={0} | all-to-all | bytes 589824 | tf_op jit(solution)/shard_map/all_to_all | solution.py:234
  56.7 2.0 %select.2 = (f32[1536,128]{1,0:T(8,128)}, s32[8,128]{1,0:T(8,128)S(1)}, s32[1,1]{1,0:T(1,128)}) custom-call(f32[576,128]{1,0:T(8,128)S(1)} %bitcast.30), custom_call_target="tpu_custom_call" | custom-call | tf_op jit(solution)/shard_map/select/pallas_call | solution.py:237
  58.6 5.6 %all-to-all-start.3 = ((f32[32,48,128]{2,1,0:T(8,128)}), f32[32,48,128]{2,1,0:T(8,128)S(1)}, u32[]{:S(2)}, u32[]{:S(2)}) async-start(f32[32,48,128]{2,1,0:T(8,128)} %bitcast.12), calls=%async_computation.3 | async-start | bytes 1572864 | tf_op jit(solution)/shard_map/all_to_all | solution.py:249
  64.9 17.2 %all-gather.3.cloned.1.call-done = f32[24,1,4,128,128]{4,3,2,1,0:T(8,128)} async-done(((f32[1,1,4,128,128]{4,3,2,1,0:T(8,128)}), f32[24,1,4,128,128]{4,3,2,1,0:T(8,128)}) %all-gather.3.cloned.1.call-update) | async-done | bytes 6291472 | tf_op jit(solution)/shard_map/all_gather | solution.py:210
  82.1 1.7 %fetch.2 = f32[16,128,128]{2,1,0:T(8,128)S(1)} custom-call(s32[8,128]{1,0:T(8,128)S(1)} %get-tuple-element.79.plan_ref, f32[96,128,128]{2,1,0:T(8,128)} %bitcast.27), custom_call_target="tpu_custom_call" | custom-call | bytes 8388608 | tf_op jit(solution)/shard_map/fetch/pallas_call | solution.py:253
  83.8 2.1 %all-to-all-done.3 = f32[32,48,128]{2,1,0:T(8,128)S(1)} async-done(((f32[32,48,128]{2,1,0:T(8,128)}), f32[32,48,128]{2,1,0:T(8,128)S(1)}, u32[]{:S(2)}, u32[]{:S(2)}) %all-to-all-start.3) | async-done | bytes 786464 | tf_op jit(solution)/shard_map/all_to_all | solution.py:249
  85.9 2.3 %conditional.1 = (f32[1,1,4,128,128]{4,3,2,1,0:T(8,128)}) conditional(s32[]{:T(128)} %convert_element_type.3, (s32[8,128]{1,0:T(8,128)S(1)}, f32[4,128,128]{2,1,0:T(8,128)S(1)}, f32[1536,128]{1,0:T(8,128)S(1)}, f32[16,128,128]{2,1,0:T(8,128)S(1)}, f32[96,128,128]{2,1,0:T(8,128)}) %tuple.39, (s32[8,128]{1,0:T(8,128)S(1)}, ...), branch_computations={%region_0.1_spmd, %region_1.4_spmd} | conditional | flops 2 | bytes 11272357 | solution.py:283
  85.9 2.3 %multiply.3 = f32[4,128,128]{2,1,0:T(8,128)} custom-call(s32[8,128]{1,0:T(8,128)S(1)} %get-tuple-element.53.plan_ref, f32[4,128,128]{2,1,0:T(8,128)S(1)} %get-tuple-element.54.base_ref, f32[1536,128]{1,0:T(8,128)S(1)} %get-tuple-element.55.got_ref, f32[16,128,128]{2,1,0:T(8,128)S(1)} %get-tuple-element.56.ahead_ref, f32[96,128,128]{2,1,0:T(8,128)} %get-tuple-element.57.x_ref), custom_call_target="tpu_custom_call" | custom-call | tf_op jit(solution)/shard_map/cond/branch_0_fun/multiply/pallas_call | solution.py:265
  (3 shorter events, 0.0 us)
Async XLA Ops:
  6.5 75.5 %all-gather.3.cloned.1.call-start = ((), (), s32[]{:S(2)}) async-start(), calls=%async_computation.4 | async-start | bytes 6553600 | tf_op jit(solution)/shard_map/all_gather | solution.py:210
  9.4 25.2 %all-to-all-start.1 = ((s32[24,1,128]{2,1,0:T(1,128)}), s32[24,1,128]{2,1,0:T(1,128)S(1)}, u32[]{:S(2)}, u32[]{:S(2)}) async-start(s32[24,1,128]{2,1,0:T(1,128)} %broadcast_in_dim.30), calls=%async_computation.1 | async-start | bytes 24576 | tf_op jit(solution)/shard_map/all_to_all | solution.py:215
  25.8 1.0 %copy-start = (f32[1,1,4,128,128]{4,3,2,1,0:T(8,128)S(1)}, f32[1,1,4,128,128]{4,3,2,1,0:T(8,128)}, u32[]{:S(2)}) copy-start(f32[1,1,4,128,128]{4,3,2,1,0:T(8,128)} %param.9) | copy-start | bytes 786436
  58.6 27.2 %all-to-all-start.3 = ((f32[32,48,128]{2,1,0:T(8,128)}), f32[32,48,128]{2,1,0:T(8,128)S(1)}, u32[]{:S(2)}, u32[]{:S(2)}) async-start(f32[32,48,128]{2,1,0:T(8,128)} %bitcast.12), calls=%async_computation.3 | async-start | bytes 1572864 | tf_op jit(solution)/shard_map/all_to_all | solution.py:249
Sparse Core Ops, SparseCore 0:
  9.8 72.2 all-gather.2

commit v5 on v4

--- a/solution.py
+++ b/solution.py
@@ -22,6 +22,13 @@
     return lax.broadcasted_iota(jnp.int32, shape, dim)
 
 
+def turned(i):
+    out = 0
+    for bit in range(5):
+        out = out + lax.rem(lax.div(i, 2**bit), 2) * 2 ** (4 - bit)
+    return out
+
+
 def dot(a, b, dims=((1,), (0,))):
     return lax.dot_general(a, b, (dims, ((), ())), preferred_element_type=jnp.float32)
 
@@ -70,7 +77,7 @@
     rows_in = CAP * piece + TABLE
     base = CAP * piece
     slots = CAP * n_row
-    my_row, my_col, first = lax.axis_index("row"), lax.axis_index("col"), 0 if initial else refs[0][0]
+    my_row, my_col, first = turned(lax.axis_index("row")), lax.axis_index("col"), 0 if initial else refs[0][0]
 
     def strided(start):
         return got_ref[pl.ds(start, n_row, stride=rows_in), :]
@@ -99,7 +106,7 @@
     table = jnp.concatenate(tables, axis=0)
     holds_row = jnp.concatenate(own_row, axis=0).astype(jnp.int32)
     holds_col = jnp.concatenate(own_col, axis=0).astype(jnp.int32)
-    inner = lax.rem(iota((slots, 1), 0), n_row) * RB + holds_row
+    inner = turned(lax.rem(iota((slots, 1), 0), n_row)) * RB + holds_row
     valid = holds_row >= 0
     wide = iota((slots, BS), 1)
     at_head = jnp.where((wide == inner) & valid, 1.0, 0.0)
@@ -231,7 +238,7 @@
         name="pack",
     )(slots, cut, base)
     parts = rows_out // 2
-    pieces = lax.all_to_all(packed.reshape(n_row, parts, 2, BS), "row", 0, 0).reshape(n_row * rows_out, BS)
+    pieces = lax.all_to_all(packed.reshape(n_row, parts, 2, BS), "row", 0, 0, axis_index_groups=[[int(format(i, "05b")[::-1], 2) for i in range(n_row)]]).reshape(n_row * rows_out, BS)
 
     def select(*first):
         chosen, plan, most = pl.pallas_call(
@@ -246,7 +253,7 @@
             compiler_params=params,
             name="select",
         )(*first, pieces)
-        tiles = lax.all_to_all(chosen.reshape(n_row, ROUND * piece, BS), "row", 0, 0)
+        tiles = lax.all_to_all(chosen.reshape(n_row, ROUND * piece, BS), "row", 0, 0, axis_index_groups=[[int(format(i, "05b")[::-1], 2) for i in range(n_row)]])
         return tiles.reshape(n_row * ROUND * piece, BS), plan, most[0, 0]
 
     def fetch(plan):

time: 95.3 us -> 95.5 us (level)
  blocking collectives: 22 us -> 23.1 us
    all_to_all x1, blocking collectives: 22 us -> 23.1 us  [per_device(): lax.all_to_all(packed.reshape(n_row, parts, 2, BS), 'row', 0, 0, axis_ind...]
where the time goes in v5:
time: 95.5 us; the launch traced here: 94.9 us
  waiting for transfers between devices  27.5 us (29%)
  blocking collectives  23.1 us (24%)
  starting transfers between devices  20.5 us (21%)
  between operations  14.8 us (15%)
  Pallas kernels  5.57 us (6%)
  local copies, waits for them, and re-layouts  2.32 us (2%)
  other arithmetic  1.12 us (1%)
    all_to_all x1, blocking collectives, per_device(): lax.all_to_all(packed.reshape(n_row, parts, 2, BS), 'row', 0, 0, axis_ind...  23.1 us
    all_gather x1, waiting for transfers between devices, per_device(): lax.all_gather(x_stack[0], 'col', axis=0, tiled=True)  16.5 us
    all_to_all x1, starting transfers between devices, per_device(): lax.all_to_all(jnp.broadcast_to(own[None, None], (n_col, 1, BS)), 'col',...  15.4 us
    all_to_all x1, waiting for transfers between devices, per_device(): lax.all_to_all(jnp.broadcast_to(own[None, None], (n_col, 1, BS)), 'col',...  7.78 us
    all_to_all x1, starting transfers between devices, select(): lax.all_to_all(chosen.reshape(n_row, ROUND * piece, BS), 'row', 0, 0, axi...  5.13 us
    all_to_all x1, waiting for transfers between devices, select(): lax.all_to_all(chosen.reshape(n_row, ROUND * piece, BS), 'row', 0, 0, axi...  2.45 us
    pallas_call x1, Pallas kernels, select(): pl.pallas_call(functools.partial(select_kernel, n_row, not first), out_sh...  1.96 us
  transfers between devices with their start and end apart: 3, of which 3 were waited for; matrix products, arithmetic and copies ran while one was open for 3% of the time, Pallas kernels for 4%

profile of v5, /device:TPU:2, one launch (start us, length us, event | category | flops | bytes accessed | tf_op | source)
XLA Modules:
  0.0 94.9 jit_solution(14233563804441725664)
XLA Ops:
  6.5 0.0 all-gather.3.cloned.1.call-start
  6.5 0.7 all-gather.3.cloned.1.call-update
  7.9 0.8 reshape.39
  8.7 0.1 pad_add_fusion
  8.7 0.6 broadcast_in_dim.30
  9.4 15.4 %all-to-all-start.1 = ((s32[24,1,128]{2,1,0:T(1,128)}), s32[24,1,128]{2,1,0:T(1,128)S(1)}, u32[]{:S(2)}, u32[]{:S(2)}) async-start(s32[24,1,128]{2,1,0:T(1,128)} %broadcast_in_dim.30), calls=%async_computation.1 | async-start | bytes 24576 | tf_op jit(solution)/shard_map/all_to_all | solution.py:222
  24.7 1.0 %bitcast_select_fusion.ahead_ref = f32[4,128,128]{2,1,0:T(8,128)S(1)} fusion(f32[1,1,4,128,128]{4,3,2,1,0:T(8,128)} %param.8, pred[4]{0:T(512)(128)(4,1)S(1)} %iota_compare_fusion), kind=kLoop, calls=%fused_computation | loop fusion | flops 131072 | bytes 524292 | tf_op jit(solution)/shard_map/jit(_where)/select_n | solution.py:220
  25.8 0.0 copy-start
  25.8 0.9 copy-done
  26.8 7.8 %all-to-all-done.1.slots_ref = s32[24,1,128]{2,1,0:T(1,128)S(1)} async-done(((s32[24,1,128]{2,1,0:T(1,128)}), s32[24,1,128]{2,1,0:T(1,128)S(1)}, u32[]{:S(2)}, u32[]{:S(2)}) %all-to-all-start.1) | async-done | bytes 12320 | tf_op jit(solution)/shard_map/all_to_all | solution.py:222
  34.5 0.1 pack.1
  34.7 23.1 %all_to_all.21 = f32[32,9,2,128]{3,2,1,0:T(2,128)S(1)} all-to-all(f32[32,9,2,128]{3,2,1,0:T(2,128)S(1)} %bitcast.25), channel_id=1, replica_groups={{0,384,192,576,96,480,288,672,48,432,240,624,144,528,336,720,24,408,216..., dimensions={0} | all-to-all | bytes 589824 | tf_op jit(solution)/shard_map/all_to_all | solution.py:241
  57.8 2.0 %select.2 = (f32[1536,128]{1,0:T(8,128)}, s32[8,128]{1,0:T(8,128)S(1)}, s32[1,1]{1,0:T(1,128)}) custom-call(f32[576,128]{1,0:T(8,128)S(1)} %bitcast.30), custom_call_target="tpu_custom_call" | custom-call | tf_op jit(solution)/shard_map/select/pallas_call | solution.py:244
  59.8 5.1 %all-to-all-start.3 = ((f32[32,48,128]{2,1,0:T(8,128)}), f32[32,48,128]{2,1,0:T(8,128)S(1)}, u32[]{:S(2)}, u32[]{:S(2)}) async-start(f32[32,48,128]{2,1,0:T(8,128)} %bitcast.12), calls=%async_computation.3 | async-start | bytes 1572864 | tf_op jit(solution)/shard_map/all_to_all | solution.py:256
  65.6 16.5 %all-gather.3.cloned.1.call-done = f32[24,1,4,128,128]{4,3,2,1,0:T(8,128)} async-done(((f32[1,1,4,128,128]{4,3,2,1,0:T(8,128)}), f32[24,1,4,128,128]{4,3,2,1,0:T(8,128)}) %all-gather.3.cloned.1.call-update) | async-done | bytes 6291472 | tf_op jit(solution)/shard_map/all_gather | solution.py:217
  82.1 1.6 %fetch.2 = f32[16,128,128]{2,1,0:T(8,128)S(1)} custom-call(s32[8,128]{1,0:T(8,128)S(1)} %get-tuple-element.79.plan_ref, f32[96,128,128]{2,1,0:T(8,128)} %bitcast.27), custom_call_target="tpu_custom_call" | custom-call | bytes 8388608 | tf_op jit(solution)/shard_map/fetch/pallas_call | solution.py:260
  83.8 2.4 %all-to-all-done.3 = f32[32,48,128]{2,1,0:T(8,128)S(1)} async-done(((f32[32,48,128]{2,1,0:T(8,128)}), f32[32,48,128]{2,1,0:T(8,128)S(1)}, u32[]{:S(2)}, u32[]{:S(2)}) %all-to-all-start.3) | async-done | bytes 786464 | tf_op jit(solution)/shard_map/all_to_all | solution.py:256
  86.2 1.8 %conditional.1 = (f32[1,1,4,128,128]{4,3,2,1,0:T(8,128)}) conditional(s32[]{:T(128)} %convert_element_type.3, (s32[8,128]{1,0:T(8,128)S(1)}, f32[4,128,128]{2,1,0:T(8,128)S(1)}, f32[1536,128]{1,0:T(8,128)S(1)}, f32[16,128,128]{2,1,0:T(8,128)S(1)}, f32[96,128,128]{2,1,0:T(8,128)}) %tuple.39, (s32[8,128]{1,0:T(8,128)S(1)}, ...), branch_computations={%region_0.1_spmd, %region_1.4_spmd} | conditional | flops 2 | bytes 11272357 | solution.py:290
  86.2 1.8 %multiply.3 = f32[4,128,128]{2,1,0:T(8,128)} custom-call(s32[8,128]{1,0:T(8,128)S(1)} %get-tuple-element.53.plan_ref, f32[4,128,128]{2,1,0:T(8,128)S(1)} %get-tuple-element.54.base_ref, f32[1536,128]{1,0:T(8,128)S(1)} %get-tuple-element.55.got_ref, f32[16,128,128]{2,1,0:T(8,128)S(1)} %get-tuple-element.56.ahead_ref, f32[96,128,128]{2,1,0:T(8,128)} %get-tuple-element.57.x_ref), custom_call_target="tpu_custom_call" | custom-call | tf_op jit(solution)/shard_map/cond/branch_0_fun/multiply/pallas_call | solution.py:272
  (3 shorter events, 0.0 us)
Async XLA Ops:
  6.5 75.6 %all-gather.3.cloned.1.call-start = ((), (), s32[]{:S(2)}) async-start(), calls=%async_computation.4 | async-start | bytes 6553600 | tf_op jit(solution)/shard_map/all_gather | solution.py:217
  9.4 25.2 %all-to-all-start.1 = ((s32[24,1,128]{2,1,0:T(1,128)}), s32[24,1,128]{2,1,0:T(1,128)S(1)}, u32[]{:S(2)}, u32[]{:S(2)}) async-start(s32[24,1,128]{2,1,0:T(1,128)} %broadcast_in_dim.30), calls=%async_computation.1 | async-start | bytes 24576 | tf_op jit(solution)/shard_map/all_to_all | solution.py:222
  25.8 1.0 %copy-start = (f32[1,1,4,128,128]{4,3,2,1,0:T(8,128)S(1)}, f32[1,1,4,128,128]{4,3,2,1,0:T(8,128)}, u32[]{:S(2)}) copy-start(f32[1,1,4,128,128]{4,3,2,1,0:T(8,128)} %param.9) | copy-start | bytes 786436
  59.8 26.4 %all-to-all-start.3 = ((f32[32,48,128]{2,1,0:T(8,128)}), f32[32,48,128]{2,1,0:T(8,128)S(1)}, u32[]{:S(2)}, u32[]{:S(2)}) async-start(f32[32,48,128]{2,1,0:T(8,128)} %bitcast.12), calls=%async_computation.3 | async-start | bytes 1572864 | tf_op jit(solution)/shard_map/all_to_all | solution.py:256
Sparse Core Ops, SparseCore 0:
  9.8 72.2 all-gather.2

commit v6 on v5

--- a/solution.py
+++ b/solution.py
@@ -125,8 +125,8 @@
     rows = jnp.concatenate(
         [jnp.concatenate([strided(e * piece + q) for e in range(CAP)], axis=0) for q in range(piece)], axis=1
     )
-    pick = jnp.concatenate([chosen.astype(jnp.bfloat16)] * 3, axis=1)
-    part = dot(pick, jnp.concatenate(split(rows, 3), axis=0))
+    pick = jnp.concatenate([chosen.astype(jnp.bfloat16)] * 2, axis=1)
+    part = dot(pick, jnp.concatenate(split(rows, 2), axis=0))
     for q in range(piece):
         for p in range(ROUND):
             out_ref[pl.ds(p * piece + q, n_row, stride=ROUND * piece), :] = part[
@@ -158,7 +158,7 @@
             n = n + used.astype(jnp.int32)
         return n
 
-    lax.fori_loop(0, plan_ref[7, 0], tile, 0)
+    return lax.fori_loop(0, plan_ref[7, 0], tile, 0)
 
 
 def fetch_kernel(plan_ref, x_ref, out_ref, sems):
@@ -170,13 +170,11 @@
         def _():
             copy(n, o, p).start()
 
-    def wait(n, o, p):
-        @pl.when(n < AHEAD)
-        def _():
-            copy(n, o, p).wait()
-
-    each_product(plan_ref, start)
-    each_product(plan_ref, wait)
+    started = each_product(plan_ref, start)
+
+    @pl.loop(0, jnp.minimum(started, AHEAD))
+    def _(n):
+        pltpu.make_async_copy(x_ref.at[0], out_ref.at[n], sems.at[n]).wait()
 
 
 def multiply_kernel(n_row, plan_ref, base_ref, got_ref, ahead_ref, x_ref, out_ref, x_buf, sem):

time: 95.5 us -> 95.9 us (level)
  no operation moved by 1% of the time
where the time goes in v6:
time: 95.9 us; the launch traced here: 95.5 us
  waiting for transfers between devices  27.3 us (28%)
  blocking collectives  23.1 us (24%)
  starting transfers between devices  20.5 us (21%)
  between operations  14.8 us (15%)
  Pallas kernels  6.31 us (7%)
  local copies, waits for them, and re-layouts  2.32 us (2%)
  other arithmetic  1.12 us (1%)
    all_to_all x1, blocking collectives, per_device(): lax.all_to_all(packed.reshape(n_row, parts, 2, BS), 'row', 0, 0, axis_ind...  23.1 us
    all_gather x1, waiting for transfers between devices, per_device(): lax.all_gather(x_stack[0], 'col', axis=0, tiled=True)  16.6 us
    all_to_all x1, starting transfers between devices, per_device(): lax.all_to_all(jnp.broadcast_to(own[None, None], (n_col, 1, BS)), 'col',...  15.4 us
    all_to_all x1, waiting for transfers between devices, per_device(): lax.all_to_all(jnp.broadcast_to(own[None, None], (n_col, 1, BS)), 'col',...  7.78 us
    all_to_all x1, starting transfers between devices, select(): lax.all_to_all(chosen.reshape(n_row, ROUND * piece, BS), 'row', 0, 0, axi...  5.13 us
    pallas_call x1, Pallas kernels, multiply(): pl.pallas_call(functools.partial(multiply_kernel, n_row), out_shape=jax.S...  2.53 us
    all_to_all x1, waiting for transfers between devices, select(): lax.all_to_all(chosen.reshape(n_row, ROUND * piece, BS), 'row', 0, 0, axi...  2.23 us
  transfers between devices with their start and end apart: 3, of which 3 were waited for; matrix products, arithmetic and copies ran while one was open for 3% of the time, Pallas kernels for 4%

profile of v6, /device:TPU:2, one launch (start us, length us, event | category | flops | bytes accessed | tf_op | source)
XLA Modules:
  0.0 95.5 jit_solution(8288943277901960219)
XLA Ops:
  6.5 0.0 all-gather.3.cloned.1.call-start
  6.5 0.7 all-gather.3.cloned.1.call-update
  7.9 0.8 reshape.39
  8.7 0.1 pad_add_fusion
  8.7 0.6 broadcast_in_dim.30
  9.4 15.4 %all-to-all-start.1 = ((s32[24,1,128]{2,1,0:T(1,128)}), s32[24,1,128]{2,1,0:T(1,128)S(1)}, u32[]{:S(2)}, u32[]{:S(2)}) async-start(s32[24,1,128]{2,1,0:T(1,128)} %broadcast_in_dim.30), calls=%async_computation.1 | async-start | bytes 24576 | tf_op jit(solution)/shard_map/all_to_all | solution.py:220
  24.7 1.0 %bitcast_select_fusion.ahead_ref = f32[4,128,128]{2,1,0:T(8,128)S(1)} fusion(f32[1,1,4,128,128]{4,3,2,1,0:T(8,128)} %param.8, pred[4]{0:T(512)(128)(4,1)S(1)} %iota_compare_fusion), kind=kLoop, calls=%fused_computation | loop fusion | flops 131072 | bytes 524292 | tf_op jit(solution)/shard_map/jit(_where)/select_n | solution.py:218
  25.8 0.0 copy-start
  25.8 0.9 copy-done
  26.8 7.8 %all-to-all-done.1.slots_ref = s32[24,1,128]{2,1,0:T(1,128)S(1)} async-done(((s32[24,1,128]{2,1,0:T(1,128)}), s32[24,1,128]{2,1,0:T(1,128)S(1)}, u32[]{:S(2)}, u32[]{:S(2)}) %all-to-all-start.1) | async-done | bytes 12320 | tf_op jit(solution)/shard_map/all_to_all | solution.py:220
  34.5 0.1 pack.1
  34.7 23.1 %all_to_all.21 = f32[32,9,2,128]{3,2,1,0:T(2,128)S(1)} all-to-all(f32[32,9,2,128]{3,2,1,0:T(2,128)S(1)} %bitcast.25), channel_id=1, replica_groups={{0,384,192,576,96,480,288,672,48,432,240,624,144,528,336,720,24,408,216..., dimensions={0} | all-to-all | bytes 589824 | tf_op jit(solution)/shard_map/all_to_all | solution.py:239
  57.8 1.9 %select.2 = (f32[1536,128]{1,0:T(8,128)}, s32[8,128]{1,0:T(8,128)S(1)}, s32[1,1]{1,0:T(1,128)}) custom-call(f32[576,128]{1,0:T(8,128)S(1)} %bitcast.30), custom_call_target="tpu_custom_call" | custom-call | tf_op jit(solution)/shard_map/select/pallas_call | solution.py:242
  59.7 5.1 %all-to-all-start.3 = ((f32[32,48,128]{2,1,0:T(8,128)}), f32[32,48,128]{2,1,0:T(8,128)S(1)}, u32[]{:S(2)}, u32[]{:S(2)}) async-start(f32[32,48,128]{2,1,0:T(8,128)} %bitcast.12), calls=%async_computation.3 | async-start | bytes 1572864 | tf_op jit(solution)/shard_map/all_to_all | solution.py:254
  65.5 16.6 %all-gather.3.cloned.1.call-done = f32[24,1,4,128,128]{4,3,2,1,0:T(8,128)} async-done(((f32[1,1,4,128,128]{4,3,2,1,0:T(8,128)}), f32[24,1,4,128,128]{4,3,2,1,0:T(8,128)}) %all-gather.3.cloned.1.call-update) | async-done | bytes 6291472 | tf_op jit(solution)/shard_map/all_gather | solution.py:215
  82.1 1.8 %fetch.2 = f32[16,128,128]{2,1,0:T(8,128)S(1)} custom-call(s32[8,128]{1,0:T(8,128)S(1)} %get-tuple-element.79.plan_ref, f32[96,128,128]{2,1,0:T(8,128)} %bitcast.27), custom_call_target="tpu_custom_call" | custom-call | bytes 8388608 | tf_op jit(solution)/shard_map/fetch/pallas_call | solution.py:258
  83.9 2.2 %all-to-all-done.3 = f32[32,48,128]{2,1,0:T(8,128)S(1)} async-done(((f32[32,48,128]{2,1,0:T(8,128)}), f32[32,48,128]{2,1,0:T(8,128)S(1)}, u32[]{:S(2)}, u32[]{:S(2)}) %all-to-all-start.3) | async-done | bytes 786464 | tf_op jit(solution)/shard_map/all_to_all | solution.py:254
  86.1 2.5 %conditional.1 = (f32[1,1,4,128,128]{4,3,2,1,0:T(8,128)}) conditional(s32[]{:T(128)} %convert_element_type.3, (s32[8,128]{1,0:T(8,128)S(1)}, f32[4,128,128]{2,1,0:T(8,128)S(1)}, f32[1536,128]{1,0:T(8,128)S(1)}, f32[16,128,128]{2,1,0:T(8,128)S(1)}, f32[96,128,128]{2,1,0:T(8,128)}) %tuple.39, (s32[8,128]{1,0:T(8,128)S(1)}, ...), branch_computations={%region_0.1_spmd, %region_1.4_spmd} | conditional | flops 2 | bytes 11272357 | solution.py:288
  86.1 2.5 %multiply.3 = f32[4,128,128]{2,1,0:T(8,128)} custom-call(s32[8,128]{1,0:T(8,128)S(1)} %get-tuple-element.53.plan_ref, f32[4,128,128]{2,1,0:T(8,128)S(1)} %get-tuple-element.54.base_ref, f32[1536,128]{1,0:T(8,128)S(1)} %get-tuple-element.55.got_ref, f32[16,128,128]{2,1,0:T(8,128)S(1)} %get-tuple-element.56.ahead_ref, f32[96,128,128]{2,1,0:T(8,128)} %get-tuple-element.57.x_ref), custom_call_target="tpu_custom_call" | custom-call | tf_op jit(solution)/shard_map/cond/branch_0_fun/multiply/pallas_call | solution.py:270
  (3 shorter events, 0.0 us)
Async XLA Ops:
  6.5 75.6 %all-gather.3.cloned.1.call-start = ((), (), s32[]{:S(2)}) async-start(), calls=%async_computation.4 | async-start | bytes 6553600 | tf_op jit(solution)/shard_map/all_gather | solution.py:215
  9.4 25.2 %all-to-all-start.1 = ((s32[24,1,128]{2,1,0:T(1,128)}), s32[24,1,128]{2,1,0:T(1,128)S(1)}, u32[]{:S(2)}, u32[]{:S(2)}) async-start(s32[24,1,128]{2,1,0:T(1,128)} %broadcast_in_dim.30), calls=%async_computation.1 | async-start | bytes 24576 | tf_op jit(solution)/shard_map/all_to_all | solution.py:220
  25.8 1.0 copy-start
  59.7 26.4 %all-to-all-start.3 = ((f32[32,48,128]{2,1,0:T(8,128)}), f32[32,48,128]{2,1,0:T(8,128)S(1)}, u32[]{:S(2)}, u32[]{:S(2)}) async-start(f32[32,48,128]{2,1,0:T(8,128)} %bitcast.12), calls=%async_computation.3 | async-start | bytes 1572864 | tf_op jit(solution)/shard_map/all_to_all | solution.py:254
Sparse Core Ops, SparseCore 0:
  9.8 72.2 all-gather.2

commit v7 on v6

--- a/solution.py
+++ b/solution.py
@@ -46,7 +46,9 @@
     rows_out = CAP * piece + TABLE
     for e in range(CAP):
         for q in range(piece):
-            out_ref[pl.ds(e * piece + q, n_row, stride=rows_out), :] = s_ref[e, q * n_row : (q + 1) * n_row, :]
+            for i in range(n_row):
+                at = int(format(i, "05b")[::-1], 2) * rows_out + e * piece + q
+                out_ref[at : at + 1, :] = s_ref[e, q * n_row + i : q * n_row + i + 1, :]
     for t in range(TABLE):
         out_ref[pl.ds(CAP * piece + t, n_row, stride=rows_out), :] = jnp.zeros((n_row, BS), jnp.float32)
 
@@ -77,7 +79,7 @@
     rows_in = CAP * piece + TABLE
     base = CAP * piece
     slots = CAP * n_row
-    my_row, my_col, first = turned(lax.axis_index("row")), lax.axis_index("col"), 0 if initial else refs[0][0]
+    my_row, my_col, first = lax.axis_index("row"), lax.axis_index("col"), 0 if initial else refs[0][0]
 
     def strided(start):
         return got_ref[pl.ds(start, n_row, stride=rows_in), :]
@@ -106,7 +108,7 @@
     table = jnp.concatenate(tables, axis=0)
     holds_row = jnp.concatenate(own_row, axis=0).astype(jnp.int32)
     holds_col = jnp.concatenate(own_col, axis=0).astype(jnp.int32)
-    inner = turned(lax.rem(iota((slots, 1), 0), n_row)) * RB + holds_row
+    inner = lax.rem(iota((slots, 1), 0), n_row) * RB + holds_row
     valid = holds_row >= 0
     wide = iota((slots, BS), 1)
     at_head = jnp.where((wide == inner) & valid, 1.0, 0.0)
@@ -121,6 +123,8 @@
     before = jnp.where(iota((slots, slots), 0) < iota((slots, slots), 1), 1.0, 0.0)
     rank = dot(need, before).astype(jnp.int32) - first
     rank = jnp.where(need > 0.5, rank, -1)
+    order = jnp.where(iota((n_row, n_row), 1) == turned(iota((n_row, n_row), 0)), 1.0, 0.0)
+    rank = dot(order, rank.astype(jnp.float32)).astype(jnp.int32)
     chosen = jnp.concatenate([jnp.where(rank == p, 1.0, 0.0) for p in range(ROUND)], axis=0)
     rows = jnp.concatenate(
         [jnp.concatenate([strided(e * piece + q) for e in range(CAP)], axis=0) for q in range(piece)], axis=1
@@ -132,13 +136,12 @@
             out_ref[pl.ds(p * piece + q, n_row, stride=ROUND * piece), :] = part[
                 p * n_row : (p + 1) * n_row, q * BS : (q + 1) * BS
             ]
-    mine = iota((n_row, BS), 0) == my_row
-
-    def own(a, n):
-        return [jnp.sum(jnp.where(mine, a[i * n_row : (i + 1) * n_row], 0.0), axis=0, keepdims=True) for i in range(n)]
-
-    own_m = jnp.concatenate(own(m, CAP) + [jnp.zeros((4, BS), jnp.float32)], axis=0)
-    own_chosen = jnp.concatenate(own(chosen, ROUND) + [jnp.zeros((BS - ROUND, BS), jnp.float32)], axis=0)
+
+    def own(a, n, at):
+        return [jnp.sum(jnp.where(iota((n_row, BS), 0) == at, a[i * n_row : (i + 1) * n_row], 0.0), axis=0, keepdims=True) for i in range(n)]
+
+    own_m = jnp.concatenate(own(m, CAP, my_row) + [jnp.zeros((4, BS), jnp.float32)], axis=0)
+    own_chosen = jnp.concatenate(own(chosen, ROUND, turned(my_row)) + [jnp.zeros((BS - ROUND, BS), jnp.float32)], axis=0)
     needed = jnp.sum(need, axis=1, keepdims=True)
     most_ref[0, 0] = (jnp.max(needed) + 0.5).astype(jnp.int32)
     here = jnp.sum(jnp.sum(own_chosen, axis=1, keepdims=True), axis=0, keepdims=True)
@@ -236,7 +239,7 @@
         name="pack",
     )(slots, cut, base)
     parts = rows_out // 2
-    pieces = lax.all_to_all(packed.reshape(n_row, parts, 2, BS), "row", 0, 0, axis_index_groups=[[int(format(i, "05b")[::-1], 2) for i in range(n_row)]]).reshape(n_row * rows_out, BS)
+    pieces = lax.all_to_all(packed.reshape(n_row, parts, 2, BS), "row", 0, 0).reshape(n_row * rows_out, BS)
 
     def select(*first):
         chosen, plan, most = pl.pallas_call(

time: 95.9 us -> 95.6 us (level)
  the two profiles are of different devices: /device:TPU:2 before, /device:TPU:16 now
where the time goes in v7:
time: 95.6 us; the launch traced here: 95.2 us
  waiting for transfers between devices  27.9 us (29%)
  blocking collectives  21.9 us (23%)
  starting transfers between devices  20.8 us (22%)
  between operations  14.8 us (15%)
  Pallas kernels  6.26 us (7%)
  local copies, waits for them, and re-layouts  2.32 us (2%)
  other arithmetic  1.12 us (1%)
    all_to_all x1, blocking collectives, per_device(): lax.all_to_all(packed.reshape(n_row, parts, 2, BS), 'row', 0, 0)  21.9 us
    all_gather x1, waiting for transfers between devices, per_device(): lax.all_gather(x_stack[0], 'col', axis=0, tiled=True)  17.2 us
    all_to_all x1, starting transfers between devices, per_device(): lax.all_to_all(jnp.broadcast_to(own[None, None], (n_col, 1, BS)), 'col',...  15.4 us
    all_to_all x1, waiting for transfers between devices, per_device(): lax.all_to_all(jnp.broadcast_to(own[None, None], (n_col, 1, BS)), 'col',...  7.62 us
    all_to_all x1, starting transfers between devices, select(): lax.all_to_all(chosen.reshape(n_row, ROUND * piece, BS), 'row', 0, 0, axi...  5.43 us
    all_to_all x1, waiting for transfers between devices, select(): lax.all_to_all(chosen.reshape(n_row, ROUND * piece, BS), 'row', 0, 0, axi...  2.4 us
    pallas_call x1, Pallas kernels, multiply(): pl.pallas_call(functools.partial(multiply_kernel, n_row), out_shape=jax.S...  2.24 us
    pallas_call x1, Pallas kernels, select(): pl.pallas_call(functools.partial(select_kernel, n_row, not first), out_sh...  1.99 us
  transfers between devices with their start and end apart: 3, of which 3 were waited for; matrix products, arithmetic and copies ran while one was open for 3% of the time, Pallas kernels for 4%

profile of v7, /device:TPU:16, one launch (start us, length us, event | category | flops | bytes accessed | tf_op | source)
XLA Modules:
  0.0 95.2 jit_solution(17161739873007182109)
XLA Ops:
  6.5 0.0 all-gather.3.cloned.1.call-start
  6.5 0.7 all-gather.3.cloned.1.call-update
  7.9 0.8 reshape.39
  8.7 0.1 pad_add_fusion
  8.7 0.6 broadcast_in_dim.30
  9.4 15.4 %all-to-all-start.1 = ((s32[24,1,128]{2,1,0:T(1,128)}), s32[24,1,128]{2,1,0:T(1,128)S(1)}, u32[]{:S(2)}, u32[]{:S(2)}) async-start(s32[24,1,128]{2,1,0:T(1,128)} %broadcast_in_dim.30), calls=%async_computation.1 | async-start | bytes 24576 | tf_op jit(solution)/shard_map/all_to_all | solution.py:223
  24.7 1.0 %bitcast_select_fusion.ahead_ref = f32[4,128,128]{2,1,0:T(8,128)S(1)} fusion(f32[1,1,4,128,128]{4,3,2,1,0:T(8,128)} %param.8, pred[4]{0:T(512)(128)(4,1)S(1)} %iota_compare_fusion), kind=kLoop, calls=%fused_computation | loop fusion | flops 131072 | bytes 524292 | tf_op jit(solution)/shard_map/jit(_where)/select_n | solution.py:221
  25.8 0.0 copy-start
  25.8 0.9 copy-done
  26.7 0.2 cut.1.cut_ref
  26.9 7.6 %all-to-all-done.1.slots_ref = s32[24,1,128]{2,1,0:T(1,128)S(1)} async-done(((s32[24,1,128]{2,1,0:T(1,128)}), s32[24,1,128]{2,1,0:T(1,128)S(1)}, u32[]{:S(2)}, u32[]{:S(2)}) %all-to-all-start.1) | async-done | bytes 12320 | tf_op jit(solution)/shard_map/all_to_all | solution.py:223
  34.5 0.1 pack.1
  34.7 21.9 %all_to_all.21 = f32[32,9,2,128]{3,2,1,0:T(2,128)S(1)} all-to-all(f32[32,9,2,128]{3,2,1,0:T(2,128)S(1)} %bitcast.25), channel_id=1, replica_groups=mesh['row'=32,'col'=24] {'row'}, dimensions={0} | all-to-all | bytes 589824 | tf_op jit(solution)/shard_map/all_to_all | solution.py:242
  56.6 2.0 %select.2 = (f32[1536,128]{1,0:T(8,128)}, s32[8,128]{1,0:T(8,128)S(1)}, s32[1,1]{1,0:T(1,128)}) custom-call(f32[576,128]{1,0:T(8,128)S(1)} %bitcast.30), custom_call_target="tpu_custom_call" | custom-call | tf_op jit(solution)/shard_map/select/pallas_call | solution.py:245
  58.6 5.4 %all-to-all-start.3 = ((f32[32,48,128]{2,1,0:T(8,128)}), f32[32,48,128]{2,1,0:T(8,128)S(1)}, u32[]{:S(2)}, u32[]{:S(2)}) async-start(f32[32,48,128]{2,1,0:T(8,128)} %bitcast.12), calls=%async_computation.3 | async-start | bytes 1572864 | tf_op jit(solution)/shard_map/all_to_all | solution.py:257
  64.7 17.2 %all-gather.3.cloned.1.call-done = f32[24,1,4,128,128]{4,3,2,1,0:T(8,128)} async-done(((f32[1,1,4,128,128]{4,3,2,1,0:T(8,128)}), f32[24,1,4,128,128]{4,3,2,1,0:T(8,128)}) %all-gather.3.cloned.1.call-update) | async-done | bytes 6291472 | tf_op jit(solution)/shard_map/all_gather | solution.py:218
  81.9 1.7 %fetch.2 = f32[16,128,128]{2,1,0:T(8,128)S(1)} custom-call(s32[8,128]{1,0:T(8,128)S(1)} %get-tuple-element.79.plan_ref, f32[96,128,128]{2,1,0:T(8,128)} %bitcast.27), custom_call_target="tpu_custom_call" | custom-call | bytes 8388608 | tf_op jit(solution)/shard_map/fetch/pallas_call | solution.py:261
  83.6 2.4 %all-to-all-done.3 = f32[32,48,128]{2,1,0:T(8,128)S(1)} async-done(((f32[32,48,128]{2,1,0:T(8,128)}), f32[32,48,128]{2,1,0:T(8,128)S(1)}, u32[]{:S(2)}, u32[]{:S(2)}) %all-to-all-start.3) | async-done | bytes 786464 | tf_op jit(solution)/shard_map/all_to_all | solution.py:257
  86.0 2.3 %conditional.1 = (f32[1,1,4,128,128]{4,3,2,1,0:T(8,128)}) conditional(s32[]{:T(128)} %convert_element_type.3, (s32[8,128]{1,0:T(8,128)S(1)}, f32[4,128,128]{2,1,0:T(8,128)S(1)}, f32[1536,128]{1,0:T(8,128)S(1)}, f32[16,128,128]{2,1,0:T(8,128)S(1)}, f32[96,128,128]{2,1,0:T(8,128)}) %tuple.39, (s32[8,128]{1,0:T(8,128)S(1)}, ...), branch_computations={%region_0.1_spmd, %region_1.4_spmd} | conditional | flops 2 | bytes 11272357 | solution.py:291
  86.0 2.2 %multiply.3 = f32[4,128,128]{2,1,0:T(8,128)} custom-call(s32[8,128]{1,0:T(8,128)S(1)} %get-tuple-element.53.plan_ref, f32[4,128,128]{2,1,0:T(8,128)S(1)} %get-tuple-element.54.base_ref, f32[1536,128]{1,0:T(8,128)S(1)} %get-tuple-element.55.got_ref, f32[16,128,128]{2,1,0:T(8,128)S(1)} %get-tuple-element.56.ahead_ref, f32[96,128,128]{2,1,0:T(8,128)} %get-tuple-element.57.x_ref), custom_call_target="tpu_custom_call" | custom-call | tf_op jit(solution)/shard_map/cond/branch_0_fun/multiply/pallas_call | solution.py:273
  (2 shorter events, 0.0 us)
Async XLA Ops:
  6.5 75.4 %all-gather.3.cloned.1.call-start = ((), (), s32[]{:S(2)}) async-start(), calls=%async_computation.4 | async-start | bytes 6553600 | tf_op jit(solution)/shard_map/all_gather | solution.py:218
  9.4 25.2 %all-to-all-start.1 = ((s32[24,1,128]{2,1,0:T(1,128)}), s32[24,1,128]{2,1,0:T(1,128)S(1)}, u32[]{:S(2)}, u32[]{:S(2)}) async-start(s32[24,1,128]{2,1,0:T(1,128)} %broadcast_in_dim.30), calls=%async_computation.1 | async-start | bytes 24576 | tf_op jit(solution)/shard_map/all_to_all | solution.py:223
  25.8 1.0 %copy-start = (f32[1,1,4,128,128]{4,3,2,1,0:T(8,128)S(1)}, f32[1,1,4,128,128]{4,3,2,1,0:T(8,128)}, u32[]{:S(2)}) copy-start(f32[1,1,4,128,128]{4,3,2,1,0:T(8,128)} %param.9) | copy-start | bytes 786436
  58.6 27.4 %all-to-all-start.3 = ((f32[32,48,128]{2,1,0:T(8,128)}), f32[32,48,128]{2,1,0:T(8,128)S(1)}, u32[]{:S(2)}, u32[]{:S(2)}) async-start(f32[32,48,128]{2,1,0:T(8,128)} %bitcast.12), calls=%async_computation.3 | async-start | bytes 1572864 | tf_op jit(solution)/shard_map/all_to_all | solution.py:257
Sparse Core Ops, SparseCore 0:
  9.8 72.0 all-gather.2

commit v8 on v5

--- a/solution.py
+++ b/solution.py
@@ -125,8 +125,8 @@
     rows = jnp.concatenate(
         [jnp.concatenate([strided(e * piece + q) for e in range(CAP)], axis=0) for q in range(piece)], axis=1
     )
-    pick = jnp.concatenate([chosen.astype(jnp.bfloat16)] * 3, axis=1)
-    part = dot(pick, jnp.concatenate(split(rows, 3), axis=0))
+    pick = jnp.concatenate([chosen.astype(jnp.bfloat16)] * 2, axis=1)
+    part = dot(pick, jnp.concatenate(split(rows, 2), axis=0))
     for q in range(piece):
         for p in range(ROUND):
             out_ref[pl.ds(p * piece + q, n_row, stride=ROUND * piece), :] = part[
@@ -183,27 +183,35 @@
     piece = BS // n_row
     out_ref[...] = base_ref[...]
 
-    def act(n, o, p):
+    def tile(p, n):
         s_tile = jnp.concatenate(
             [got_ref[pl.ds(p * piece + q, n_row, stride=ROUND * piece), :] for q in range(piece)], axis=0
         )
         s_high, s_low = split(s_tile, 2)
 
-        @pl.when(n < AHEAD)
-        def _():
-            x_buf[...] = ahead_ref[jnp.minimum(n, AHEAD - 1)]
-
-        @pl.when(n >= AHEAD)
-        def _():
-            copy = pltpu.make_async_copy(x_ref.at[plan_ref[o, p] - 1], x_buf, sem)
-            copy.start()
-            copy.wait()
-
-        x_high, x_low = split(x_buf[...], 2)
-        product = dot(x_high, s_high) + (dot(x_high, s_low) + dot(x_low, s_high))
-        out_ref[o] = out_ref[o] - 0.5 * product
-
-    each_product(plan_ref, act)
+        def subtract(o, x):
+            x_high, x_low = split(x, 2)
+            product = dot(x_high, s_high) + (dot(x_high, s_low) + dot(x_low, s_high))
+            out_ref[o] = out_ref[o] - 0.5 * product
+
+        for o in range(CAP):
+            used = plan_ref[o, p] > 0
+
+            @pl.when(used & (n < AHEAD))
+            def _(n=n):
+                subtract(o, ahead_ref[jnp.minimum(n, AHEAD - 1)])
+
+            @pl.when(used & (n >= AHEAD))
+            def _():
+                copy = pltpu.make_async_copy(x_ref.at[plan_ref[o, p] - 1], x_buf, sem)
+                copy.start()
+                copy.wait()
+                subtract(o, x_buf[...])
+
+            n = n + used.astype(jnp.int32)
+        return n
+
+    lax.fori_loop(0, plan_ref[7, 0], tile, 0)
 
 
 def per_device(n_row, n_col, x_stack, s_stack, entries, counts):

time: 95.5 us -> 96.1 us (level)
  no operation moved by 1% of the time
where the time goes in v8:
time: 96.1 us; the launch traced here: 95.7 us
  waiting for transfers between devices  27.3 us (28%)
  blocking collectives  23.1 us (24%)
  starting transfers between devices  20.5 us (21%)
  between operations  14.8 us (15%)
  Pallas kernels  6.52 us (7%)
  local copies, waits for them, and re-layouts  2.32 us (2%)
  other arithmetic  1.12 us (1%)
    all_to_all x1, blocking collectives, per_device(): lax.all_to_all(packed.reshape(n_row, parts, 2, BS), 'row', 0, 0, axis_ind...  23.1 us
    all_gather x1, waiting for transfers between devices, per_device(): lax.all_gather(x_stack[0], 'col', axis=0, tiled=True)  16.6 us
    all_to_all x1, starting transfers between devices, per_device(): lax.all_to_all(jnp.broadcast_to(own[None, None], (n_col, 1, BS)), 'col',...  15.4 us
    all_to_all x1, waiting for transfers between devices, per_device(): lax.all_to_all(jnp.broadcast_to(own[None, None], (n_col, 1, BS)), 'col',...  7.78 us
    all_to_all x1, starting transfers between devices, select(): lax.all_to_all(chosen.reshape(n_row, ROUND * piece, BS), 'row', 0, 0, axi...  5.13 us
    pallas_call x1, Pallas kernels, multiply(): pl.pallas_call(functools.partial(multiply_kernel, n_row), out_shape=jax.S...  2.71 us
    all_to_all x1, waiting for transfers between devices, select(): lax.all_to_all(chosen.reshape(n_row, ROUND * piece, BS), 'row', 0, 0, axi...  2.2 us
  transfers between devices with their start and end apart: 3, of which 3 were waited for; matrix products, arithmetic and copies ran while one was open for 3% of the time, Pallas kernels for 4%

profile of v8, /device:TPU:2, one launch (start us, length us, event | category | flops | bytes accessed | tf_op | source)
XLA Modules:
  0.0 95.7 jit_solution(14164833816800418181)
XLA Ops:
  6.5 0.0 all-gather.3.cloned.1.call-start
  6.5 0.7 all-gather.3.cloned.1.call-update
  7.9 0.8 reshape.39
  8.7 0.1 pad_add_fusion
  8.7 0.6 broadcast_in_dim.30
  9.4 15.4 %all-to-all-start.1 = ((s32[24,1,128]{2,1,0:T(1,128)}), s32[24,1,128]{2,1,0:T(1,128)S(1)}, u32[]{:S(2)}, u32[]{:S(2)}) async-start(s32[24,1,128]{2,1,0:T(1,128)} %broadcast_in_dim.30), calls=%async_computation.1 | async-start | bytes 24576 | tf_op jit(solution)/shard_map/all_to_all | solution.py:230
  24.7 1.0 %bitcast_select_fusion.ahead_ref = f32[4,128,128]{2,1,0:T(8,128)S(1)} fusion(f32[1,1,4,128,128]{4,3,2,1,0:T(8,128)} %param.8, pred[4]{0:T(512)(128)(4,1)S(1)} %iota_compare_fusion), kind=kLoop, calls=%fused_computation | loop fusion | flops 131072 | bytes 524292 | tf_op jit(solution)/shard_map/jit(_where)/select_n | solution.py:228
  25.8 0.0 copy-start
  25.8 0.9 copy-done
  26.8 7.8 %all-to-all-done.1.slots_ref = s32[24,1,128]{2,1,0:T(1,128)S(1)} async-done(((s32[24,1,128]{2,1,0:T(1,128)}), s32[24,1,128]{2,1,0:T(1,128)S(1)}, u32[]{:S(2)}, u32[]{:S(2)}) %all-to-all-start.1) | async-done | bytes 12320 | tf_op jit(solution)/shard_map/all_to_all | solution.py:230
  34.5 0.1 pack.1
  34.7 23.1 %all_to_all.21 = f32[32,9,2,128]{3,2,1,0:T(2,128)S(1)} all-to-all(f32[32,9,2,128]{3,2,1,0:T(2,128)S(1)} %bitcast.25), channel_id=1, replica_groups={{0,384,192,576,96,480,288,672,48,432,240,624,144,528,336,720,24,408,216..., dimensions={0} | all-to-all | bytes 589824 | tf_op jit(solution)/shard_map/all_to_all | solution.py:249
  57.8 1.9 %select.2 = (f32[1536,128]{1,0:T(8,128)}, s32[8,128]{1,0:T(8,128)S(1)}, s32[1,1]{1,0:T(1,128)}) custom-call(f32[576,128]{1,0:T(8,128)S(1)} %bitcast.30), custom_call_target="tpu_custom_call" | custom-call | tf_op jit(solution)/shard_map/select/pallas_call | solution.py:252
  59.7 5.1 %all-to-all-start.3 = ((f32[32,48,128]{2,1,0:T(8,128)}), f32[32,48,128]{2,1,0:T(8,128)S(1)}, u32[]{:S(2)}, u32[]{:S(2)}) async-start(f32[32,48,128]{2,1,0:T(8,128)} %bitcast.12), calls=%async_computation.3 | async-start | bytes 1572864 | tf_op jit(solution)/shard_map/all_to_all | solution.py:264
  65.5 16.6 %all-gather.3.cloned.1.call-done = f32[24,1,4,128,128]{4,3,2,1,0:T(8,128)} async-done(((f32[1,1,4,128,128]{4,3,2,1,0:T(8,128)}), f32[24,1,4,128,128]{4,3,2,1,0:T(8,128)}) %all-gather.3.cloned.1.call-update) | async-done | bytes 6291472 | tf_op jit(solution)/shard_map/all_gather | solution.py:225
  82.1 1.8 %fetch.2 = f32[16,128,128]{2,1,0:T(8,128)S(1)} custom-call(s32[8,128]{1,0:T(8,128)S(1)} %get-tuple-element.79.plan_ref, f32[96,128,128]{2,1,0:T(8,128)} %bitcast.27), custom_call_target="tpu_custom_call" | custom-call | bytes 8388608 | tf_op jit(solution)/shard_map/fetch/pallas_call | solution.py:268
  83.9 2.2 %all-to-all-done.3 = f32[32,48,128]{2,1,0:T(8,128)S(1)} async-done(((f32[32,48,128]{2,1,0:T(8,128)}), f32[32,48,128]{2,1,0:T(8,128)S(1)}, u32[]{:S(2)}, u32[]{:S(2)}) %all-to-all-start.3) | async-done | bytes 786464 | tf_op jit(solution)/shard_map/all_to_all | solution.py:264
  86.1 2.7 %conditional.1 = (f32[1,1,4,128,128]{4,3,2,1,0:T(8,128)}) conditional(s32[]{:T(128)} %convert_element_type.3, (s32[8,128]{1,0:T(8,128)S(1)}, f32[4,128,128]{2,1,0:T(8,128)S(1)}, f32[1536,128]{1,0:T(8,128)S(1)}, f32[16,128,128]{2,1,0:T(8,128)S(1)}, f32[96,128,128]{2,1,0:T(8,128)}) %tuple.39, (s32[8,128]{1,0:T(8,128)S(1)}, ...), branch_computations={%region_0.1_spmd, %region_1.4_spmd} | conditional | flops 2 | bytes 11272357 | solution.py:298
  86.1 2.7 %multiply.3 = f32[4,128,128]{2,1,0:T(8,128)} custom-call(s32[8,128]{1,0:T(8,128)S(1)} %get-tuple-element.53.plan_ref, f32[4,128,128]{2,1,0:T(8,128)S(1)} %get-tuple-element.54.base_ref, f32[1536,128]{1,0:T(8,128)S(1)} %get-tuple-element.55.got_ref, f32[16,128,128]{2,1,0:T(8,128)S(1)} %get-tuple-element.56.ahead_ref, f32[96,128,128]{2,1,0:T(8,128)} %get-tuple-element.57.x_ref), custom_call_target="tpu_custom_call" | custom-call | tf_op jit(solution)/shard_map/cond/branch_0_fun/multiply/pallas_call | solution.py:280
  (3 shorter events, 0.0 us)
Async XLA Ops:
  6.5 75.6 %all-gather.3.cloned.1.call-start = ((), (), s32[]{:S(2)}) async-start(), calls=%async_computation.4 | async-start | bytes 6553600 | tf_op jit(solution)/shard_map/all_gather | solution.py:225
  9.4 25.2 %all-to-all-start.1 = ((s32[24,1,128]{2,1,0:T(1,128)}), s32[24,1,128]{2,1,0:T(1,128)S(1)}, u32[]{:S(2)}, u32[]{:S(2)}) async-start(s32[24,1,128]{2,1,0:T(1,128)} %broadcast_in_dim.30), calls=%async_computation.1 | async-start | bytes 24576 | tf_op jit(solution)/shard_map/all_to_all | solution.py:230
  25.8 1.0 copy-start
  59.7 26.4 %all-to-all-start.3 = ((f32[32,48,128]{2,1,0:T(8,128)}), f32[32,48,128]{2,1,0:T(8,128)S(1)}, u32[]{:S(2)}, u32[]{:S(2)}) async-start(f32[32,48,128]{2,1,0:T(8,128)} %bitcast.12), calls=%async_computation.3 | async-start | bytes 1572864 | tf_op jit(solution)/shard_map/all_to_all | solution.py:264
Sparse Core Ops, SparseCore 0:
  9.8 72.2 all-gather.2

commit v9 on v7

--- a/solution.py
+++ b/solution.py
@@ -184,27 +184,35 @@
     piece = BS // n_row
     out_ref[...] = base_ref[...]
 
-    def act(n, o, p):
+    def tile(p, n):
         s_tile = jnp.concatenate(
             [got_ref[pl.ds(p * piece + q, n_row, stride=ROUND * piece), :] for q in range(piece)], axis=0
         )
         s_high, s_low = split(s_tile, 2)
 
-        @pl.when(n < AHEAD)
-        def _():
-            x_buf[...] = ahead_ref[jnp.minimum(n, AHEAD - 1)]
-
-        @pl.when(n >= AHEAD)
-        def _():
-            copy = pltpu.make_async_copy(x_ref.at[plan_ref[o, p] - 1], x_buf, sem)
-            copy.start()
-            copy.wait()
-
-        x_high, x_low = split(x_buf[...], 2)
-        product = dot(x_high, s_high) + (dot(x_high, s_low) + dot(x_low, s_high))
-        out_ref[o] = out_ref[o] - 0.5 * product
-
-    each_product(plan_ref, act)
+        def subtract(o, x):
+            x_high, x_low = split(x, 2)
+            product = dot(x_high, s_high) + (dot(x_high, s_low) + dot(x_low, s_high))
+            out_ref[o] = out_ref[o] - 0.5 * product
+
+        for o in range(CAP):
+            used = plan_ref[o, p] > 0
+
+            @pl.when(used & (n < AHEAD))
+            def _(n=n):
+                subtract(o, ahead_ref[jnp.minimum(n, AHEAD - 1)])
+
+            @pl.when(used & (n >= AHEAD))
+            def _():
+                copy = pltpu.make_async_copy(x_ref.at[plan_ref[o, p] - 1], x_buf, sem)
+                copy.start()
+                copy.wait()
+                subtract(o, x_buf[...])
+
+            n = n + used.astype(jnp.int32)
+        return n
+
+    lax.fori_loop(0, plan_ref[7, 0], tile, 0)
 
 
 def per_device(n_row, n_col, x_stack, s_stack, entries, counts):

time: 95.6 us -> 95.7 us (level)
  no operation moved by 1% of the time
where the time goes in v9:
time: 95.7 us; the launch traced here: 94.5 us
  waiting for transfers between devices  28 us (29%)
  blocking collectives  21.9 us (23%)
  starting transfers between devices  20.8 us (22%)
  between operations  14.8 us (15%)
  Pallas kernels  5.48 us (6%)
  local copies, waits for them, and re-layouts  2.32 us (2%)
  other arithmetic  1.12 us (1%)
    all_to_all x1, blocking collectives, per_device(): lax.all_to_all(packed.reshape(n_row, parts, 2, BS), 'row', 0, 0)  21.9 us
    all_gather x1, waiting for transfers between devices, per_device(): lax.all_gather(x_stack[0], 'col', axis=0, tiled=True)  17.2 us
    all_to_all x1, starting transfers between devices, per_device(): lax.all_to_all(jnp.broadcast_to(own[None, None], (n_col, 1, BS)), 'col',...  15.4 us
    all_to_all x1, waiting for transfers between devices, per_device(): lax.all_to_all(jnp.broadcast_to(own[None, None], (n_col, 1, BS)), 'col',...  7.62 us
    all_to_all x1, starting transfers between devices, select(): lax.all_to_all(chosen.reshape(n_row, ROUND * piece, BS), 'row', 0, 0, axi...  5.43 us
    all_to_all x1, waiting for transfers between devices, select(): lax.all_to_all(chosen.reshape(n_row, ROUND * piece, BS), 'row', 0, 0, axi...  2.5 us
    pallas_call x1, Pallas kernels, select(): pl.pallas_call(functools.partial(select_kernel, n_row, not first), out_sh...  1.99 us
  transfers between devices with their start and end apart: 3, of which 3 were waited for; matrix products, arithmetic and copies ran while one was open for 3% of the time, Pallas kernels for 4%

profile of v9, /device:TPU:16, one launch (start us, length us, event | category | flops | bytes accessed | tf_op | source)
XLA Modules:
  0.0 94.5 jit_solution(10381440790034074540)
XLA Ops:
  6.5 0.0 all-gather.3.cloned.1.call-start
  6.5 0.7 all-gather.3.cloned.1.call-update
  7.9 0.8 reshape.39
  8.7 0.1 pad_add_fusion
  8.7 0.6 broadcast_in_dim.30
  9.4 15.4 %all-to-all-start.1 = ((s32[24,1,128]{2,1,0:T(1,128)}), s32[24,1,128]{2,1,0:T(1,128)S(1)}, u32[]{:S(2)}, u32[]{:S(2)}) async-start(s32[24,1,128]{2,1,0:T(1,128)} %broadcast_in_dim.30), calls=%async_computation.1 | async-start | bytes 24576 | tf_op jit(solution)/shard_map/all_to_all | solution.py:231
  24.7 1.0 %bitcast_select_fusion.ahead_ref = f32[4,128,128]{2,1,0:T(8,128)S(1)} fusion(f32[1,1,4,128,128]{4,3,2,1,0:T(8,128)} %param.8, pred[4]{0:T(512)(128)(4,1)S(1)} %iota_compare_fusion), kind=kLoop, calls=%fused_computation | loop fusion | flops 131072 | bytes 524292 | tf_op jit(solution)/shard_map/jit(_where)/select_n | solution.py:229
  25.8 0.0 copy-start
  25.8 0.9 copy-done
  26.7 0.2 cut.1.cut_ref
  26.9 7.6 %all-to-all-done.1.slots_ref = s32[24,1,128]{2,1,0:T(1,128)S(1)} async-done(((s32[24,1,128]{2,1,0:T(1,128)}), s32[24,1,128]{2,1,0:T(1,128)S(1)}, u32[]{:S(2)}, u32[]{:S(2)}) %all-to-all-start.1) | async-done | bytes 12320 | tf_op jit(solution)/shard_map/all_to_all | solution.py:231
  34.5 0.1 pack.1
  34.7 21.9 %all_to_all.21 = f32[32,9,2,128]{3,2,1,0:T(2,128)S(1)} all-to-all(f32[32,9,2,128]{3,2,1,0:T(2,128)S(1)} %bitcast.25), channel_id=1, replica_groups=mesh['row'=32,'col'=24] {'row'}, dimensions={0} | all-to-all | bytes 589824 | tf_op jit(solution)/shard_map/all_to_all | solution.py:250
  56.6 2.0 %select.2 = (f32[1536,128]{1,0:T(8,128)}, s32[8,128]{1,0:T(8,128)S(1)}, s32[1,1]{1,0:T(1,128)}) custom-call(f32[576,128]{1,0:T(8,128)S(1)} %bitcast.30), custom_call_target="tpu_custom_call" | custom-call | tf_op jit(solution)/shard_map/select/pallas_call | solution.py:253
  58.6 5.4 %all-to-all-start.3 = ((f32[32,48,128]{2,1,0:T(8,128)}), f32[32,48,128]{2,1,0:T(8,128)S(1)}, u32[]{:S(2)}, u32[]{:S(2)}) async-start(f32[32,48,128]{2,1,0:T(8,128)} %bitcast.12), calls=%async_computation.3 | async-start | bytes 1572864 | tf_op jit(solution)/shard_map/all_to_all | solution.py:265
  64.7 17.2 %all-gather.3.cloned.1.call-done = f32[24,1,4,128,128]{4,3,2,1,0:T(8,128)} async-done(((f32[1,1,4,128,128]{4,3,2,1,0:T(8,128)}), f32[24,1,4,128,128]{4,3,2,1,0:T(8,128)}) %all-gather.3.cloned.1.call-update) | async-done | bytes 6291472 | tf_op jit(solution)/shard_map/all_gather | solution.py:226
  81.9 1.6 %fetch.2 = f32[16,128,128]{2,1,0:T(8,128)S(1)} custom-call(s32[8,128]{1,0:T(8,128)S(1)} %get-tuple-element.79.plan_ref, f32[96,128,128]{2,1,0:T(8,128)} %bitcast.27), custom_call_target="tpu_custom_call" | custom-call | bytes 8388608 | tf_op jit(solution)/shard_map/fetch/pallas_call | solution.py:269
  83.5 2.5 %all-to-all-done.3 = f32[32,48,128]{2,1,0:T(8,128)S(1)} async-done(((f32[32,48,128]{2,1,0:T(8,128)}), f32[32,48,128]{2,1,0:T(8,128)S(1)}, u32[]{:S(2)}, u32[]{:S(2)}) %all-to-all-start.3) | async-done | bytes 786464 | tf_op jit(solution)/shard_map/all_to_all | solution.py:265
  86.0 1.6 %conditional.1 = (f32[1,1,4,128,128]{4,3,2,1,0:T(8,128)}) conditional(s32[]{:T(128)} %convert_element_type.3, (s32[8,128]{1,0:T(8,128)S(1)}, f32[4,128,128]{2,1,0:T(8,128)S(1)}, f32[1536,128]{1,0:T(8,128)S(1)}, f32[16,128,128]{2,1,0:T(8,128)S(1)}, f32[96,128,128]{2,1,0:T(8,128)}) %tuple.39, (s32[8,128]{1,0:T(8,128)S(1)}, ...), branch_computations={%region_0.1_spmd, %region_1.4_spmd} | conditional | flops 2 | bytes 11272357 | solution.py:299
  86.0 1.6 %multiply.3 = f32[4,128,128]{2,1,0:T(8,128)} custom-call(s32[8,128]{1,0:T(8,128)S(1)} %get-tuple-element.53.plan_ref, f32[4,128,128]{2,1,0:T(8,128)S(1)} %get-tuple-element.54.base_ref, f32[1536,128]{1,0:T(8,128)S(1)} %get-tuple-element.55.got_ref, f32[16,128,128]{2,1,0:T(8,128)S(1)} %get-tuple-element.56.ahead_ref, f32[96,128,128]{2,1,0:T(8,128)} %get-tuple-element.57.x_ref), custom_call_target="tpu_custom_call" | custom-call | tf_op jit(solution)/shard_map/cond/branch_0_fun/multiply/pallas_call | solution.py:281
  (2 shorter events, 0.0 us)
Async XLA Ops:
  6.5 75.4 %all-gather.3.cloned.1.call-start = ((), (), s32[]{:S(2)}) async-start(), calls=%async_computation.4 | async-start | bytes 6553600 | tf_op jit(solution)/shard_map/all_gather | solution.py:226
  9.4 25.2 %all-to-all-start.1 = ((s32[24,1,128]{2,1,0:T(1,128)}), s32[24,1,128]{2,1,0:T(1,128)S(1)}, u32[]{:S(2)}, u32[]{:S(2)}) async-start(s32[24,1,128]{2,1,0:T(1,128)} %broadcast_in_dim.30), calls=%async_computation.1 | async-start | bytes 24576 | tf_op jit(solution)/shard_map/all_to_all | solution.py:231
  25.8 1.0 %copy-start = (f32[1,1,4,128,128]{4,3,2,1,0:T(8,128)S(1)}, f32[1,1,4,128,128]{4,3,2,1,0:T(8,128)}, u32[]{:S(2)}) copy-start(f32[1,1,4,128,128]{4,3,2,1,0:T(8,128)} %param.9) | copy-start | bytes 786436
  58.6 27.4 %all-to-all-start.3 = ((f32[32,48,128]{2,1,0:T(8,128)}), f32[32,48,128]{2,1,0:T(8,128)S(1)}, u32[]{:S(2)}, u32[]{:S(2)}) async-start(f32[32,48,128]{2,1,0:T(8,128)} %bitcast.12), calls=%async_computation.3 | async-start | bytes 1572864 | tf_op jit(solution)/shard_map/all_to_all | solution.py:265
Sparse Core Ops, SparseCore 0:
  9.8 72.0 all-gather.2
